TPU v7x, 32 devices: a whole 2x2x4 slice. The times are simulated.
32 devices in a mesh: leaf: 4 (over z), row: 2 (over y), col: 4 (over x, core).
Axes of the slice: x: 2, y: 2, z: 4, core: 2. Of those that a mesh axis runs over, the one named last changes fastest.
Arguments:
- front: bfloat16 [4, 8192, 8192], P('leaf', 'row', 'col'), may hold values from -6 to 6
- child_tiles: bfloat16 [4, 2, 1536, 6144], P('leaf', None, 'row', 'col'), may hold values from -0.9 to 0.9
- child_rows: int32 [4, 2, 1536], P('leaf', None, 'row'), may hold values from 0 to 8191, as said below
- child_cols: int32 [4, 2, 6144], P('leaf', None, 'col'), may hold values from 0 to 8191, as said below
- shift: float32 [4, 8192], P('leaf'), may hold values from 16.9705627 to 33.941125
- pivot_tiles: int32 [4, 64], P('leaf'), may hold values from 0 to 63, each once within a row
Outputs:
- factored: bfloat16 [4, 8192, 8192], P('leaf', 'row', 'col')
Inputs may be any that keep to these rules, and one draw needn't show every extreme that they name: For each l and b, the entries k of child_rows[l, b] with k // 768 = r are distinct and lie in [r * 4096, (r + 1) * 4096). For each l and b, the entries k of child_cols[l, b] with k // 1536 = c are distinct and lie in [c * 2048, (c + 1) * 2048).
All inputs are finite; a program needn't handle non-finite values.
Results may differ from a plain program's by a relative error of at most 0.0065.
Values may be sent and summed in bfloat16 or wider, within the bound.
A program may use at most 192 MiB of HBM per device.

v0:
```python
import jax
import jax.numpy as jnp
from jax import lax
from jax.sharding import PartitionSpec as P

PB = 512
TB = 128
PANELS = 2


def swapped(block, axis, distance):
    count = lax.axis_size(axis)
    route = []
    for low in range(count):
        high = low | 1 << distance
        if high != low and high < count:
            route += [(low, high), (high, low)]
    return lax.ppermute(block, axis, route)


def invert_block(diag_block):
    gram = jnp.dot(diag_block.T, diag_block, precision=lax.Precision.HIGHEST)
    factor = jnp.linalg.cholesky(gram)
    return jax.scipy.linalg.cho_solve((factor, True), diag_block.T)


def slot_table(local_idx, length):
    entries = local_idx.shape[0]
    return (
        jnp.full((length,), -1, jnp.int32).at[local_idx].set(jnp.arange(entries, dtype=jnp.int32))
    )


def spread(arrived, row_local, col_local, rows_dev, cols_dev):
    row_slots = slot_table(row_local, rows_dev)
    col_slots = slot_table(col_local, cols_dev)
    picked = jnp.take(arrived, jnp.maximum(row_slots, 0), axis=0)
    picked = jnp.take(picked, jnp.maximum(col_slots, 0), axis=1)
    landed = (row_slots >= 0)[:, None] & (col_slots >= 0)[None, :]
    return jnp.where(landed, picked, jnp.zeros((), jnp.bfloat16))


def shards(front, child_tiles, child_rows, child_cols, shift, pivot_tiles):
    local_block = front[0]
    rows_dev, cols_dev = local_block.shape
    row_start = lax.axis_index("row") * rows_dev
    col_start = lax.axis_index("col") * cols_dev
    landed_parts = []
    for bit_level in range(2):
        arrived = swapped(child_tiles[0, bit_level], "leaf", bit_level)
        landed_parts.append(
            spread(
                arrived,
                child_rows[0, bit_level] - row_start,
                child_cols[0, bit_level] - col_start,
                rows_dev,
                cols_dev,
            )
        )
    summed = (
        local_block.astype(jnp.float32)
        + landed_parts[0].astype(jnp.float32)
        + landed_parts[1].astype(jnp.float32)
    )
    matrix = summed.astype(jnp.bfloat16)
    shift_row = shift[0]
    pivot_order = pivot_tiles[0]
    offsets = jnp.arange(TB, dtype=jnp.int32)
    row_tile = (row_start + jnp.arange(rows_dev, dtype=jnp.int32)) // TB
    col_tile = (col_start + jnp.arange(cols_dev, dtype=jnp.int32)) // TB
    keep_rows = jnp.ones((rows_dev,), dtype=bool)
    keep_cols = jnp.ones((cols_dev,), dtype=bool)
    per_panel = PB // TB
    zero_value = jnp.zeros((), jnp.bfloat16)
    for panel_num in range(PANELS):
        panel_tiles = pivot_order[panel_num * per_panel : (panel_num + 1) * per_panel]
        pivot_index = (panel_tiles[:, None] * TB + offsets[None, :]).reshape(-1)
        col_local = pivot_index - col_start
        inside_cols = (col_local >= 0) & (col_local < cols_dev)
        col_clip = jnp.clip(col_local, 0, cols_dev - 1)
        row_local = pivot_index - row_start
        inside_rows = (row_local >= 0) & (row_local < rows_dev)
        row_clip = jnp.clip(row_local, 0, rows_dev - 1)
        colpart = jnp.where(inside_cols[None, :], jnp.take(matrix, col_clip, axis=1), zero_value)
        rowpart = jnp.where(inside_rows[:, None], jnp.take(matrix, row_clip, axis=0), zero_value)
        columns = lax.psum(colpart, "col").astype(jnp.float32).astype(jnp.bfloat16)
        panel_rows = lax.psum(rowpart, "row").astype(jnp.float32).astype(jnp.bfloat16)
        corner = jnp.where(inside_cols[None, :], jnp.take(panel_rows, col_clip, axis=1), zero_value)
        diag_block = lax.psum(corner, "col").astype(jnp.float32)
        diag_block = diag_block + jnp.diag(shift_row[pivot_index])
        inverse_half = invert_block(diag_block).astype(jnp.bfloat16)
        multipliers = jnp.dot(columns, inverse_half, preferred_element_type=jnp.float32).astype(
            jnp.bfloat16
        )
        update = jnp.dot(multipliers, panel_rows, preferred_element_type=jnp.float32)
        keep_rows = keep_rows & ~jnp.any(row_tile[:, None] == panel_tiles[None, :], axis=1)
        keep_cols = keep_cols & ~jnp.any(col_tile[:, None] == panel_tiles[None, :], axis=1)
        lowered = (matrix.astype(jnp.float32) - update).astype(jnp.bfloat16)
        matrix = jnp.where(keep_rows[:, None] & keep_cols[None, :], lowered, matrix)
    return matrix[None]


def solution(mesh):
    in_specs = (
        P("leaf", "row", "col"),
        P("leaf", None, "row", "col"),
        P("leaf", None, "row"),
        P("leaf", None, "col"),
        P("leaf", None),
        P("leaf", None),
    )
    out_specs = P("leaf", "row", "col")
    return jax.shard_map(shards, mesh=mesh, in_specs=in_specs, out_specs=out_specs, check_vma=False)
```

profile of v0, /device:TPU:0, one launch (start us, length us, event | category | flops | bytes accessed | tf_op | source)
XLA Modules:
  0.0 1069.8 jit_solution(1723839831926213292)
XLA Ops:
  6.6 4.9 slice_bitcast_fusion.1
  11.5 3.0 collective-permute-start
  14.5 2.6 collective-permute-start.1
  17.2 3.4 scatter_custom_fusion
  20.6 6.2 scatter_custom_fusion.1
  26.8 3.4 scatter_custom_fusion.2
  30.2 6.4 scatter_custom_fusion.3
  40.8 75.7 %collective-permute-done = bf16[768,1536]{1,0:T(8,128)(2,1)} collective-permute-done((bf16[768,1536]{1,0:T(8,128)(2,1)}, bf16[768,1536]{1,0:T(8,128)(2,1)}, u32[]{:S(2)}, u32[]{:S(2)}) %collective-permute-start) | collective-permute-done | bytes 2359328 | tf_op jit(solution)/shard_map/ppermute | solution.py:18
  116.5 27.2 %gather_fusion.2 = bf16[4096,1536]{1,0:T(8,128)(2,1)} fusion(bf16[768,1536]{1,0:T(8,128)(2,1)} %collective-permute-done, s32[4096]{0:T(1024)S(1)} %maximum_clamp_fusion.1), kind=kCustom, calls=%fused_computation.clone | custom fusion | bytes 25182208 | tf_op jit(solution)/shard_map/jit(_take)/gather | solution.py:37
  143.7 11.2 %broadcast_select_fusion.1 = bf16[4096,1536]{1,0:T(8,128)(2,1)} fusion(bf16[4096,1536]{1,0:T(8,128)(2,1)} %gather_fusion.2, pred[4096]{0:T(1024)(128)(4,1)S(1)} %get-tuple-element.91), kind=kLoop, calls=%fused_computation.31 | loop fusion | flops 6291456 | bytes 25169920 | tf_op jit(solution)/shard_map/jit(_take)/select_n | solution.py:37
  154.9 16.7 %copy.27 = bf16[4096,1536]{0,1:T(8,128)(2,1)} copy(bf16[4096,1536]{1,0:T(8,128)(2,1)} %broadcast_select_fusion.1) | data formatting | bytes 25165824 | tf_op jit(solution)/shard_map/jit(_take)/select_n | solution.py:37
  171.6 34.8 %gather_fusion.3 = bf16[2048,4096]{1,0:T(8,128)(2,1)} fusion(bf16[4096,1536]{0,1:T(8,128)(2,1)} %copy.27, s32[2048]{0:T(1024)S(1)} %maximum_clamp_fusion.3), kind=kCustom, calls=%fused_computation.1.clone | custom fusion | bytes 33562624 | tf_op jit(solution)/shard_map/jit(_take)/gather | solution.py:38
  206.4 22.6 %copy.28 = bf16[2048,4096]{0,1:T(8,128)(2,1)} copy(bf16[2048,4096]{1,0:T(8,128)(2,1)} %gather_fusion.3) | data formatting | bytes 33554432 | tf_op jit(solution)/shard_map/jit(_take)/gather | solution.py:38
  229.0 19.0 %gather_fusion.4 = bf16[4096,1536]{1,0:T(8,128)(2,1)} fusion(bf16[768,1536]{1,0:T(8,128)(2,1)S(1)} %collective-permute-done.1, s32[4096]{0:T(1024)S(1)} %maximum_clamp_fusion), kind=kCustom, calls=%fused_computation.5.clone | custom fusion | bytes 25182208 | tf_op jit(solution)/shard_map/jit(_take)/gather | solution.py:37
  248.0 11.2 %broadcast_select_fusion = bf16[4096,1536]{1,0:T(8,128)(2,1)} fusion(bf16[4096,1536]{1,0:T(8,128)(2,1)} %gather_fusion.4, pred[4096]{0:T(1024)(128)(4,1)S(1)} %get-tuple-element.93), kind=kLoop, calls=%fused_computation.30 | loop fusion | flops 6291456 | bytes 25169920 | tf_op jit(solution)/shard_map/jit(_take)/select_n | solution.py:37
  259.2 16.7 %copy.29 = bf16[4096,1536]{0,1:T(8,128)(2,1)} copy(bf16[4096,1536]{1,0:T(8,128)(2,1)} %broadcast_select_fusion) | data formatting | bytes 25165824 | tf_op jit(solution)/shard_map/jit(_take)/select_n | solution.py:37
  275.9 34.8 %gather_fusion.5 = bf16[2048,4096]{1,0:T(8,128)(2,1)} fusion(bf16[4096,1536]{0,1:T(8,128)(2,1)} %copy.29, s32[2048]{0:T(1024)S(1)} %maximum_clamp_fusion.2), kind=kCustom, calls=%fused_computation.6.clone | custom fusion | bytes 33562624 | tf_op jit(solution)/shard_map/jit(_take)/gather | solution.py:38
  310.7 22.6 %copy.30 = bf16[2048,4096]{0,1:T(8,128)(2,1)} copy(bf16[2048,4096]{1,0:T(8,128)(2,1)} %gather_fusion.5) | data formatting | bytes 33554432 | tf_op jit(solution)/shard_map/jit(_take)/gather | solution.py:38
  333.4 28.4 %fusion.1 = bf16[4096,2048]{1,0:T(8,128)(2,1)} fusion(bf16[1,4096,2048]{2,1,0:T(8,128)(2,1)} %param.19, bf16[2048,4096]{0,1:T(8,128)(2,1)} %copy.30, bf16[2048,4096]{0,1:T(8,128)(2,1)} %copy.28, pred[2048]{0:T(1024)(128)(4,1)S(1)} %copy-done.8, pred[2048]{0:T(1024)(128)(4,1)S(1)} %copy-done.9, pred[2048]{0:T(1024)(128)(4,1)S(1)} %copy-done.7, ...), kind=kLoop, calls=%fused_computation.22 | loop fusion | flops 100663296 | bytes 67125248 | tf_op jit(solution)/shard_map/convert_element_type | solution.py:65
  361.8 12.3 %gather_fusion.7 = bf16[512,2048]{1,0:T(8,128)(2,1)S(1)} fusion(bf16[4096,2048]{1,0:T(8,128)(2,1)} %fusion.1, s32[1024]{0:T(1024)S(1)} %copy-done.6), kind=kCustom, calls=%fused_computation.3.clone | custom fusion | bytes 4196352 | tf_op jit(solution)/shard_map/jit(_take)/gather | solution.py:85
  374.2 1.7 select_select_fusion.1
  376.0 21.2 %copy.31 = bf16[4096,2048]{0,1:T(8,128)(2,1)} copy(bf16[4096,2048]{1,0:T(8,128)(2,1)} %fusion.1) | data formatting | bytes 33554432 | tf_op jit(solution)/shard_map/convert_element_type | solution.py:65
  397.2 16.6 %gather_fusion.6 = bf16[512,4096]{1,0:T(8,128)(2,1)} fusion(bf16[4096,2048]{0,1:T(8,128)(2,1)} %copy.31, s32[1024]{0:T(1024)S(1)} %pad_clamp_fusion.5), kind=kCustom, calls=%fused_computation.2.clone | custom fusion | bytes 8390656 | tf_op jit(solution)/shard_map/jit(_take)/gather | solution.py:84
  413.8 4.4 bitcast_select_fusion.1
  418.2 21.1 %all-reduce.8.cloned.1.call-done = bf16[512,2048]{1,0:T(8,128)(2,1)} async-done(((bf16[512,2048]{1,0:T(8,128)(2,1)}), bf16[512,2048]{1,0:T(8,128)(2,1)}) %all-reduce.8.cloned.1.call-update) | async-done | bytes 2097168 | tf_op jit(solution)/shard_map/psum | solution.py:87
  439.3 2.9 copy.32
  442.1 2.0 gather_fusion.8
  445.3 3.3 gather_fusion
  449.3 90.3 %all-reduce.14.cloned.1.call-done = (bf16[4096,512]{0,1:T(8,128)(2,1)}, bf16[512,512]{0,1:T(8,128)(2,1)}) async-done(((bf16[4096,512]{0,1:T(8,128)(2,1)}, bf16[512,512]{0,1:T(8,128)(2,1)}), (bf16[4096,512]{0,1:T(8,128)(2,1)}, bf16[512,512]{0,1:T(8,128)(2,1)})) %all-reduce.14.cloned.1.call-update) | async-done | bytes 4718608 | tf_op jit(solution)/shard_map/psum | solution.py:86
  539.5 3.1 fusion.8
  545.3 11.7 %cholesky.286 = f32[128,128]{1,0:T(8,128)S(1)} custom-call(f32[128,128]{1,0:T(8,128)S(1)} %cholesky.426), custom_call_target="Cholesky" | custom-call | tf_op jit(solution)/shard_map/jit(cholesky)/cholesky | solution.py:23
  557.2 9.8 custom-call.29
  569.6 11.9 %cholesky.305 = f32[128,128]{1,0:T(8,128)S(1)} custom-call(f32[128,128]{1,0:T(8,128)S(1)} %cholesky.430), custom_call_target="Cholesky" | custom-call | tf_op jit(solution)/shard_map/jit(cholesky)/cholesky | solution.py:23
  582.8 9.8 custom-call.30
  594.2 11.7 %cholesky.326 = f32[128,128]{1,0:T(8,128)S(1)} custom-call(f32[128,128]{1,0:T(8,128)S(1)} %cholesky.435), custom_call_target="Cholesky" | custom-call | tf_op jit(solution)/shard_map/jit(cholesky)/cholesky | solution.py:23
  606.6 9.8 custom-call.31
  617.9 12.1 %cholesky.343 = f32[128,128]{1,0:T(8,128)S(1)} custom-call(f32[128,128]{1,0:T(8,128)S(1)} %convolution_subtract_fusion.17), custom_call_target="Cholesky" | custom-call | tf_op jit(solution)/shard_map/jit(cholesky)/cholesky | solution.py:23
  633.5 7.7 while.4
  641.2 39.3 %custom-call.32 = f32[4,128,128]{1,2,0:T(8,128)S(1)} custom-call(f32[4,128,128]{2,1,0:T(8,128)S(1)} %get-tuple-element.26), custom_call_target="InvertDiagBlocksLowerTriangular" | custom-call | tf_op jit(solution)/shard_map/jit(_cho_solve)/triangular_solve | solution.py:24
  686.8 26.0 %and_select_fusion.2 = bf16[4096,2048]{1,0:T(8,128)(2,1)} fusion(bf16[4096,2048]{1,0:T(8,128)(2,1)} %fusion.1, pred[2048]{0:T(1024)(128)(4,1)S(1)} %get-tuple-element.101, pred[4096]{0:T(1024)(128)(4,1)S(1)} %get-tuple-element.99, bf16[512,2048]{1,0:T(8,128)(2,1)} %all-reduce.8.cloned.1.call-done, bf16[4096,512]{0,1:T(8,128)(2,1)} %get-tuple-element.54, ...), kind=kOutput, calls=%fused_computation.27 | convolution fusion | flops 10783555584 | bytes 40769536 | tf_op jit(solution)/shard_map/dot_general | solution.py:95
  712.8 12.3 %gather_fusion.10 = bf16[512,2048]{1,0:T(8,128)(2,1)S(1)} fusion(bf16[4096,2048]{1,0:T(8,128)(2,1)} %and_select_fusion.2, s32[1024]{0:T(1024)S(1)} %pad_clamp_fusion.1), kind=kCustom, calls=%fused_computation.8.clone | custom fusion | bytes 4196352 | tf_op jit(solution)/shard_map/jit(_take)/gather | solution.py:85
  725.1 1.7 select_select_fusion
  726.9 21.0 %copy.34 = bf16[4096,2048]{0,1:T(8,128)(2,1)} copy(bf16[4096,2048]{1,0:T(8,128)(2,1)} %and_select_fusion.2) | data formatting | bytes 33554432 | tf_op jit(solution)/shard_map/jit(_where)/select_n | solution.py:99
  747.9 16.6 %gather_fusion.9 = bf16[512,4096]{1,0:T(8,128)(2,1)} fusion(bf16[4096,2048]{0,1:T(8,128)(2,1)} %copy.34, s32[1024]{0:T(1024)S(1)} %pad_clamp_fusion.2), kind=kCustom, calls=%fused_computation.7.clone | custom fusion | bytes 8390656 | tf_op jit(solution)/shard_map/jit(_take)/gather | solution.py:84
  764.5 4.4 bitcast_select_fusion
  768.9 21.1 %all-reduce.10.cloned.1.call-done = bf16[512,2048]{1,0:T(8,128)(2,1)} async-done(((bf16[512,2048]{1,0:T(8,128)(2,1)}), bf16[512,2048]{1,0:T(8,128)(2,1)}) %all-reduce.10.cloned.1.call-update) | async-done | bytes 2097168 | tf_op jit(solution)/shard_map/psum | solution.py:87
  790.0 2.9 copy.35
  792.9 2.0 gather_fusion.11
  796.0 3.5 gather_fusion.1
  799.6 90.7 %all-reduce.12.cloned.1.call-done = (bf16[4096,512]{0,1:T(8,128)(2,1)}, bf16[512,512]{0,1:T(8,128)(2,1)}) async-done(((bf16[4096,512]{0,1:T(8,128)(2,1)}, bf16[512,512]{0,1:T(8,128)(2,1)}), (bf16[4096,512]{0,1:T(8,128)(2,1)}, bf16[512,512]{0,1:T(8,128)(2,1)})) %all-reduce.12.cloned.1.call-update) | async-done | bytes 4718608 | tf_op jit(solution)/shard_map/psum | solution.py:86
  890.3 3.1 fusion.6
  896.1 11.7 %cholesky.358 = f32[128,128]{1,0:T(8,128)S(1)} custom-call(f32[128,128]{1,0:T(8,128)S(1)} %cholesky.439), custom_call_target="Cholesky" | custom-call | tf_op jit(solution)/shard_map/jit(cholesky)/cholesky | solution.py:23
  908.0 9.8 custom-call.33
  920.3 11.9 %cholesky.377 = f32[128,128]{1,0:T(8,128)S(1)} custom-call(f32[128,128]{1,0:T(8,128)S(1)} %cholesky.443), custom_call_target="Cholesky" | custom-call | tf_op jit(solution)/shard_map/jit(cholesky)/cholesky | solution.py:23
  933.5 9.8 custom-call.34
  944.9 11.7 %cholesky.398 = f32[128,128]{1,0:T(8,128)S(1)} custom-call(f32[128,128]{1,0:T(8,128)S(1)} %cholesky.448), custom_call_target="Cholesky" | custom-call | tf_op jit(solution)/shard_map/jit(cholesky)/cholesky | solution.py:23
  957.3 9.8 custom-call.35
  968.5 11.9 %cholesky.415 = f32[128,128]{1,0:T(8,128)S(1)} custom-call(f32[128,128]{1,0:T(8,128)S(1)} %convolution_subtract_fusion.16), custom_call_target="Cholesky" | custom-call | tf_op jit(solution)/shard_map/jit(cholesky)/cholesky | solution.py:23
  983.9 7.8 while.5
  984.5 1.3 bitcast_dynamic-update-slice_fusion.5
  988.4 1.3 bitcast_dynamic-update-slice_fusion.5
  990.4 1.3 bitcast_dynamic-update-slice_fusion.5
  991.7 39.3 %custom-call.36 = f32[4,128,128]{1,2,0:T(8,128)S(1)} custom-call(f32[4,128,128]{2,1,0:T(8,128)S(1)} %get-tuple-element.27), custom_call_target="InvertDiagBlocksLowerTriangular" | custom-call | tf_op jit(solution)/shard_map/jit(_cho_solve)/triangular_solve | solution.py:24
  1037.2 25.8 %fusion.2 = bf16[1,4096,2048]{2,1,0:T(8,128)(2,1)} fusion(bf16[4096,2048]{1,0:T(8,128)(2,1)} %and_select_fusion.2, pred[2048]{0:T(1024)(128)(4,1)S(1)} %get-tuple-element.100, pred[4096]{0:T(1024)(128)(4,1)S(1)} %get-tuple-element.98, bf16[512,2048]{1,0:T(8,128)(2,1)} %all-reduce.10.cloned.1.call-done, bf16[4096,512]{0,1:T(8,128)(2,1)} %get-tuple-element.52, ...), kind=kOutput, calls=%fused_computation.29 | convolution fusion | flops 10783555584 | bytes 40769536 | tf_op jit(solution)/shard_map/dot_general | solution.py:95
  (188 shorter events, 53.7 us)
Async XLA Ops:
  6.5 438.8 %copy-start = (f32[1,8192]{1,0:T(1,128)S(1)}, f32[1,8192]{1,0:T(1,128)}, u32[]{:S(2)}) copy-start(f32[1,8192]{1,0:T(1,128)} %param.23) | copy-start | bytes 98308
  6.5 10.5 copy-start.5
  6.5 10.6 copy-start.17
  6.5 30.0 %copy-start.12 = (s32[1,64]{1,0:T(1,128)S(1)}, s32[1,64]{1,0:T(1,128)}, u32[]{:S(2)}) copy-start(s32[1,64]{1,0:T(1,128)} %param.24) | copy-start | bytes 772
  6.5 432.7 %all-reduce.8.cloned.1.call-start = ((), (), s32[]{:S(2)}) async-start(), calls=%async_computation | async-start | bytes 4194304 | tf_op jit(solution)/shard_map/psum | solution.py:87
  11.5 105.0 %collective-permute-start = (bf16[768,1536]{1,0:T(8,128)(2,1)}, bf16[768,1536]{1,0:T(8,128)(2,1)}, u32[]{:S(2)}, u32[]{:S(2)}) collective-permute-start(bf16[768,1536]{1,0:T(8,128)(2,1)} %get-tuple-element.68), channel_id=1, source_target_pairs={{0,8},{8,0},{16,24},{24,16},{1,9},{9,1},{17,25},{25,17},{2,10},{10... | collective-permute-start | bytes 7077896 | tf_op jit(solution)/shard_map/ppermute | solution.py:18
  14.5 214.5 %collective-permute-start.1 = (bf16[768,1536]{1,0:T(8,128)(2,1)}, bf16[768,1536]{1,0:T(8,128)(2,1)S(1)}, u32[]{:S(2)}, u32[]{:S(2)}) collective-permute-start(bf16[768,1536]{1,0:T(8,128)(2,1)} %get-tuple-element.69), channel_id=1, source_target_pairs={{0,16},{16,0},{8,24},{24,8},{1,17},{17,1},{9,25},{25,9},{2,18},{18... | collective-permute-start | bytes 7077896 | tf_op jit(solution)/shard_map/ppermute | solution.py:18
  37.2 1.9 copy-start.15
  310.7 22.6 %copy-start.3 = (pred[4096]{0:T(1024)(128)(4,1)S(1)}, pred[4096]{0:T(1024)(128)(4,1)}, u32[]{:S(2)}) copy-start(pred[4096]{0:T(1024)(128)(4,1)} %get-tuple-element.90) | copy-start | bytes 12292
  310.7 22.6 %copy-start.4 = (pred[4096]{0:T(1024)(128)(4,1)S(1)}, pred[4096]{0:T(1024)(128)(4,1)}, u32[]{:S(2)}) copy-start(pred[4096]{0:T(1024)(128)(4,1)} %get-tuple-element.92) | copy-start | bytes 12292
  310.7 22.6 %copy-start.7 = (pred[2048]{0:T(1024)(128)(4,1)S(1)}, pred[2048]{0:T(1024)(128)(4,1)}, u32[]{:S(2)}) copy-start(pred[2048]{0:T(1024)(128)(4,1)} %get-tuple-element.96) | copy-start | bytes 6148
  310.7 22.6 %copy-start.8 = (pred[2048]{0:T(1024)(128)(4,1)S(1)}, pred[2048]{0:T(1024)(128)(4,1)}, u32[]{:S(2)}) copy-start(pred[2048]{0:T(1024)(128)(4,1)} %get-tuple-element.97) | copy-start | bytes 6148
  310.7 22.6 %copy-start.9 = (pred[2048]{0:T(1024)(128)(4,1)S(1)}, pred[2048]{0:T(1024)(128)(4,1)}, u32[]{:S(2)}) copy-start(pred[2048]{0:T(1024)(128)(4,1)} %get-tuple-element.118) | copy-start | bytes 6148
  310.7 22.6 %copy-start.10 = (pred[2048]{0:T(1024)(128)(4,1)S(1)}, pred[2048]{0:T(1024)(128)(4,1)}, u32[]{:S(2)}) copy-start(pred[2048]{0:T(1024)(128)(4,1)} %get-tuple-element.119) | copy-start | bytes 6148
  333.4 28.5 %copy-start.6 = (s32[1024]{0:T(1024)S(1)}, s32[1024]{0:T(1024)}, u32[]{:S(2)}) copy-start(s32[1024]{0:T(1024)} %pad_clamp_fusion.4) | copy-start | bytes 12292
  361.8 12.4 %copy-start.20 = (pred[512]{0:T(512)(128)(4,1)S(1)}, pred[512]{0:T(512)(128)(4,1)}, u32[]{:S(2)}) copy-start(pred[512]{0:T(512)(128)(4,1)} %get-tuple-element.109) | copy-start | bytes 1540
  361.8 12.4 %copy-start.21 = (pred[512]{0:T(512)(128)(4,1)S(1)}, pred[512]{0:T(512)(128)(4,1)}, u32[]{:S(2)}) copy-start(pred[512]{0:T(512)(128)(4,1)} %get-tuple-element.110) | copy-start | bytes 1540
  361.8 14.1 %copy-start.11 = (s32[512]{0:T(512)S(1)}, s32[512]{0:T(512)}, u32[]{:S(2)}) copy-start(s32[512]{0:T(512)} %get-tuple-element.61) | copy-start | bytes 6148
  375.9 163.6 %all-reduce.14.cloned.1.call-start = ((), (), s32[]{:S(2)}) async-start(), calls=%async_computation.3 | async-start | bytes 9437184 | tf_op jit(solution)/shard_map/psum | solution.py:86
  397.2 16.6 %copy-start.18 = (pred[512]{0:T(512)(128)(4,1)S(1)}, pred[512]{0:T(512)(128)(4,1)}, u32[]{:S(2)}) copy-start(pred[512]{0:T(512)(128)(4,1)} %get-tuple-element.108) | copy-start | bytes 1540
  397.2 16.6 %copy-start.19 = (pred[512]{0:T(512)(128)(4,1)S(1)}, pred[512]{0:T(512)(128)(4,1)}, u32[]{:S(2)}) copy-start(pred[512]{0:T(512)(128)(4,1)} %get-tuple-element.60) | copy-start | bytes 1540
  418.2 27.0 %copy-start.16 = (s32[4]{0:T(128)S(1)}, s32[4]{0:T(128)}, u32[]{:S(2)}) copy-start(s32[4]{0:T(128)} %copy-done.15) | copy-start | bytes 52
  418.2 30.4 %copy-start.14 = (s32[4]{0:T(128)S(1)}, s32[4]{0:T(128)}, u32[]{:S(2)}) copy-start(s32[4]{0:T(128)} %get-tuple-element.106) | copy-start | bytes 52
  418.2 30.6 %copy-start.13 = (s32[1,64]{1,0:T(1,128)S(1)}, s32[1,64]{1,0:T(1,128)}, u32[]{:S(2)}) copy-start(s32[1,64]{1,0:T(1,128)} %param.24) | copy-start | bytes 772
  445.2 344.9 %all-reduce.10.cloned.1.call-start = ((), (), s32[]{:S(2)}) async-start(), calls=%async_computation.1 | async-start | bytes 4194304 | tf_op jit(solution)/shard_map/psum | solution.py:87
  448.6 184.8 %copy-start.22 = (s32[4]{0:T(128)S(1)}, s32[4]{0:T(128)}, u32[]{:S(2)}) copy-start(s32[4]{0:T(128)} %get-tuple-element.120) | copy-start | bytes 52
  544.3 1.0 copy-start.1
  726.8 163.5 %all-reduce.12.cloned.1.call-start = ((), (), s32[]{:S(2)}) async-start(), calls=%async_computation.2 | async-start | bytes 9437184 | tf_op jit(solution)/shard_map/psum | solution.py:86
  895.1 1.0 copy-start.2
Sparse Core Ops, SparseCore 0:
  376.0 63.1 all-reduce.7
  445.3 94.1 all-reduce.13
  726.9 63.0 all-reduce.9
  796.0 94.1 all-reduce.11
where the time goes:
time: 1080 us; the launch traced here: 1070 us
  local copies, waits for them, and re-layouts  354 us (33%)
  other arithmetic  311 us (29%)
  waiting for transfers between devices  299 us (28%)
  matrix products  81.1 us (8%)
  between operations  19.4 us (2%)
    psum x2, waiting for transfers between devices, shards(): columns = lax.psum(colpart, 'col').astype(jnp.float32).astype(jnp.bfloat16)  181 us
    another operation x30, other arithmetic, invert_block(): factor = jnp.linalg.cholesky(gram)  159 us
    gather x4, local copies, waits for them, and re-layouts, spread(): picked = jnp.take(picked, jnp.maximum(col_slots, 0), axis=1)  115 us
    another operation x4, other arithmetic, invert_block(): return jax.scipy.linalg.cho_solve((factor, True), diag_block.T)  78.9 us
    ppermute x2, waiting for transfers between devices, swapped(): return lax.ppermute(block, axis, route)  75.7 us
    dot_general x2, matrix products, shards(): jnp.dot(multipliers, panel_rows, preferred_element_type=jnp.float32)  51.8 us
    gather x2, local copies, waits for them, and re-layouts, spread(): picked = jnp.take(arrived, jnp.maximum(row_slots, 0), axis=0)  46.2 us
    psum x2, waiting for transfers between devices, shards(): lax.psum(rowpart, 'row').astype(jnp.float32).astype(jnp.bfloat16)  42.2 us
  transfers between devices with their start and end apart: 6, of which 5 were waited for; matrix products, arithmetic and copies ran while one was open for 21% of the time, Pallas kernels for 0%

commit v1 on v0

v1 whole, which is shorter than its diff:
```python
import functools

import jax
import jax.numpy as jnp
from jax import lax
from jax.experimental import pallas as pl
from jax.experimental.pallas import tpu as pltpu
from jax.sharding import PartitionSpec as P

PB = 512
TB = 128
PANELS = 2
BF16 = jnp.bfloat16
F32 = jnp.float32
VMEM_LIMIT = 48 * 1024 * 1024


def params(*semantics):
    return pltpu.CompilerParams(dimension_semantics=semantics or None, vmem_limit_bytes=VMEM_LIMIT)


def mm(a, b):
    return jnp.dot(a, b, preferred_element_type=F32)


def swapped(block, axis, distance):
    count = lax.axis_size(axis)
    route = []
    for low in range(count):
        high = low | 1 << distance
        if high != low and high < count:
            route += [(low, high), (high, low)]
    return lax.ppermute(block, axis, route)


def widen_kernel(width, cols_ref, tile_ref, out_ref):
    base = pl.program_id(0) * width
    lane = lax.broadcasted_iota(jnp.int32, cols_ref.shape, 1)
    delta = cols_ref[...] - base
    picks = [jnp.where(delta == lane + g * TB, 1.0, 0.0).astype(BF16) for g in range(width // TB)]
    out_ref[...] = mm(tile_ref[...], jnp.concatenate(picks, axis=1)).astype(BF16)


def widen(tile, col_local, cols_dev):
    height, entries = tile.shape
    width = min(512, cols_dev)
    spread_cols = jnp.broadcast_to(col_local[:, None], (entries, TB))
    return pl.pallas_call(
        functools.partial(widen_kernel, width),
        grid=(cols_dev // width,),
        in_specs=[
            pl.BlockSpec((entries, TB), lambda j: (0, 0)),
            pl.BlockSpec((height, entries), lambda j: (0, 0)),
        ],
        out_specs=pl.BlockSpec((height, width), lambda j: (0, j)),
        out_shape=jax.ShapeDtypeStruct((height, cols_dev), BF16),
        compiler_params=params("arbitrary"),
        cost_estimate=pl.CostEstimate(
            flops=2 * height * entries * cols_dev, bytes_accessed=8 << 20, transcendentals=0
        ),
        name="widen",
    )(spread_cols, tile)


def assemble_kernel(high, row0_ref, row1_ref, wide0_ref, wide1_ref, front_ref, out_ref):
    base = pl.program_id(0) * high
    entries = row0_ref.shape[1]
    line = lax.broadcasted_iota(jnp.int32, (high, entries), 0) + base
    pick0 = jnp.where(row0_ref[...] == line, 1.0, 0.0).astype(BF16)
    pick1 = jnp.where(row1_ref[...] == line, 1.0, 0.0).astype(BF16)
    cols = out_ref.shape[1]
    step = min(512, cols)
    for start in range(0, cols, step):
        part = slice(start, start + step)
        landed = mm(pick0, wide0_ref[:, part]) + mm(pick1, wide1_ref[:, part])
        out_ref[:, part] = (front_ref[:, part].astype(F32) + landed).astype(BF16)


def assemble(front, wide, row_local):
    rows, cols = front.shape
    entries = wide[0].shape[0]
    high = min(512, rows)
    whole = pl.BlockSpec((entries, cols), lambda i: (0, 0))
    index = pl.BlockSpec((1, entries), lambda i: (0, 0))
    block = pl.BlockSpec((high, cols), lambda i: (i, 0))
    return pl.pallas_call(
        functools.partial(assemble_kernel, high),
        grid=(rows // high,),
        in_specs=[index, index, whole, whole, block],
        out_specs=block,
        out_shape=jax.ShapeDtypeStruct((rows, cols), BF16),
        compiler_params=params("arbitrary"),
        cost_estimate=pl.CostEstimate(
            flops=4 * rows * entries * cols, bytes_accessed=4 * rows * cols, transcendentals=0
        ),
        name="assemble",
    )(row_local[0][None], row_local[1][None], wide[0], wide[1], front)


def strip_kernel(place_ref, inside_ref, in_ref, out_ref):
    held = inside_ref[pl.program_id(0)] > 0

    @pl.when(held)
    def _():
        out_ref[...] = in_ref[...]

    @pl.when(jnp.logical_not(held))
    def _():
        out_ref[...] = jnp.zeros_like(out_ref)


def strip(matrix, place, inside, by_rows, name):
    rows, cols = matrix.shape
    count = place.shape[0]
    if by_rows:
        spec = pl.BlockSpec((TB, cols), lambda q, place, inside: (place[q], 0))
        out = pl.BlockSpec((TB, cols), lambda q, place, inside: (q, 0))
        shape = (count * TB, cols)
    else:
        spec = pl.BlockSpec((rows, TB), lambda q, place, inside: (0, place[q]))
        out = pl.BlockSpec((rows, TB), lambda q, place, inside: (0, q))
        shape = (rows, count * TB)
    return pl.pallas_call(
        strip_kernel,
        grid_spec=pltpu.PrefetchScalarGridSpec(
            num_scalar_prefetch=2, grid=(count,), in_specs=[spec], out_specs=out
        ),
        out_shape=jax.ShapeDtypeStruct(shape, BF16),
        compiler_params=params("arbitrary"),
        cost_estimate=pl.CostEstimate(
            flops=0, bytes_accessed=4 * shape[0] * shape[1], transcendentals=0
        ),
        name=name,
    )(place, inside, matrix)


def newton_inverse(block, shift_row, x_ref):
    size = block.shape[0]
    down = lax.broadcasted_iota(jnp.int32, (size, size), 0)
    across = lax.broadcasted_iota(jnp.int32, (size, size), 1)
    diagonal = down == across
    wide = block.astype(F32)
    full = jnp.where(diagonal, wide + shift_row, wide)
    center = jnp.sum(jnp.where(diagonal, full, 0.0), axis=1, keepdims=True)
    off = jnp.where(diagonal, 0.0, wide).astype(BF16)
    half = full.astype(BF16)
    gram = lax.dot_general(half, half, (((1,), (1,)), ((), ())), preferred_element_type=F32)
    scale = 1.5 / jnp.max(jnp.sum(jnp.abs(gram), axis=1, keepdims=True))
    x_ref[...] = full.T * scale

    def coarse(state):
        count, norm, _ = state
        x = x_ref[...]
        x_half = x.astype(BF16)
        rest = jnp.where(diagonal, 1.0, 0.0) - mm(half, x_half)
        x_ref[...] = x + mm(x_half, rest.astype(BF16))
        return count + 1, jnp.sum(rest * rest), norm

    def coarse_on(state):
        count, norm, before = state
        return (count < 40) & (norm > 1.0) & (norm < before)

    state = (jnp.int32(0), jnp.float32(1e30), jnp.float32(2e30))
    _, norm, _ = lax.while_loop(coarse_on, coarse, state)

    @pl.when(jnp.logical_not(norm < 4.0))
    def _():
        x_ref[...] = full.T * scale

    def fine(state):
        count, _ = state
        x = x_ref[...]
        x_half = x.astype(BF16)
        x_low = (x - x_half.astype(F32)).astype(BF16)
        rest = jnp.where(diagonal, 1.0, 0.0) - (mm(off, x_half) + mm(off, x_low) + center * x)
        rest_half = rest.astype(BF16)
        rest_low = (rest - rest_half.astype(F32)).astype(BF16)
        x_ref[...] = x + (mm(x_half, rest_half) + mm(x_low, rest_half) + mm(x_half, rest_low))
        return count + 1, jnp.sum(rest * rest)

    def fine_on(state):
        count, norm = state
        return (count < 64) & jnp.logical_not(norm < 1e-4)

    lax.while_loop(fine_on, fine, (jnp.int32(0), jnp.float32(1e30)))
    return x_ref[...].astype(BF16)


def invert_kernel(diag_ref, shift_ref, inv0_ref, inv1_ref, x_ref):
    inv0 = newton_inverse(diag_ref[:PB, :PB], shift_ref[:, :PB], x_ref)
    inv0_ref[...] = inv0
    below = mm(diag_ref[PB:, :PB], inv0).astype(BF16)
    second = diag_ref[PB:, PB:].astype(F32) - mm(below, diag_ref[:PB, PB:])
    inv1_ref[...] = newton_inverse(second.astype(BF16), shift_ref[:, PB:], x_ref)


def invert(diag, shift_row):
    return pl.pallas_call(
        invert_kernel,
        out_shape=[jax.ShapeDtypeStruct((PB, PB), BF16)] * 2,
        scratch_shapes=[pltpu.VMEM((PB, PB), F32)],
        compiler_params=params(),
        cost_estimate=pl.CostEstimate(flops=60 << 30, bytes_accessed=4 << 20, transcendentals=0),
        name="invert",
    )(diag, shift_row)


def eliminate_kernel(
    blocks, half_ref, near_ref, far_ref, front_ref, rows_ref, diag_ref, inv0_ref, inv1_ref,
    keep_row_ref, keep_col_ref, out_ref, right, left,
):
    i = pl.program_id(0)
    inv0 = inv0_ref[...]
    cols = out_ref.shape[1]
    step = min(512, cols)

    @pl.when(i == 0)
    def _():
        below = mm(diag_ref[PB:, :PB], inv0).astype(BF16)
        for start in range(0, cols, step):
            part = slice(start, start + step)
            first = rows_ref[:PB, part]
            second = rows_ref[PB:, part].astype(F32) - mm(below, first)
            right[:PB, part] = (first.astype(F32) * keep_col_ref[0:1, part]).astype(BF16)
            right[PB:, part] = (
                second.astype(BF16).astype(F32) * keep_col_ref[1:2, part]
            ).astype(BF16)

    mine = (i // blocks) == half_ref[0]

    def factors(strip_ref):
        first = mm(strip_ref[:, :PB], inv0).astype(BF16)
        lowered = strip_ref[:, PB:].astype(F32) - mm(first, diag_ref[:PB, PB:])
        second = mm(lowered.astype(BF16), inv1_ref[...]).astype(BF16)
        left[:, :PB] = (first.astype(F32) * keep_row_ref[:, 0:1]).astype(BF16)
        left[:, PB:] = (second.astype(F32) * keep_row_ref[:, 1:2]).astype(BF16)

    @pl.when(mine)
    def _():
        factors(near_ref)

    @pl.when(jnp.logical_not(mine))
    def _():
        factors(far_ref)

    for start in range(0, cols, step):
        part = slice(start, start + step)
        update = mm(left[...], right[:, part])
        out_ref[:, part] = (front_ref[:, part].astype(F32) - update).astype(BF16)


def eliminate(near, far, half, matrix, panel_rows, diag, inv0, inv1, keep_row, keep_col):
    rows, cols = matrix.shape
    depth = near.shape[1]
    high = min(512, near.shape[0])
    blocks = near.shape[0] // high
    fixed = lambda shape: pl.BlockSpec(shape, lambda i, half: (0, 0))
    strip_spec = pl.BlockSpec((high, depth), lambda i, half: (lax.rem(i, blocks), 0))
    block = pl.BlockSpec((high, cols), lambda i, half: (i, 0))
    return pl.pallas_call(
        functools.partial(eliminate_kernel, blocks),
        grid_spec=pltpu.PrefetchScalarGridSpec(
            num_scalar_prefetch=1,
            grid=(rows // high,),
            in_specs=[
                strip_spec,
                strip_spec,
                block,
                fixed((depth, cols)),
                fixed((depth, depth)),
                fixed((PB, PB)),
                fixed((PB, PB)),
                pl.BlockSpec((high, 2), lambda i, half: (i, 0)),
                fixed((2, cols)),
            ],
            out_specs=block,
            scratch_shapes=[pltpu.VMEM((depth, cols), BF16), pltpu.VMEM((high, depth), BF16)],
        ),
        out_shape=jax.ShapeDtypeStruct((rows, cols), BF16),
        compiler_params=params("arbitrary"),
        cost_estimate=pl.CostEstimate(
            flops=2 * rows * depth * cols, bytes_accessed=6 * rows * cols, transcendentals=0
        ),
        name="eliminate",
    )(half, near, far, matrix, panel_rows, diag, inv0, inv1, keep_row, keep_col)


def summed_halves(part):
    count = lax.axis_size("col")
    rows = part.shape[0] // 2
    which = lax.axis_index("col") & 1
    kept = lax.dynamic_slice_in_dim(part, which * rows, rows, 0)
    sent = lax.dynamic_slice_in_dim(part, (1 - which) * rows, rows, 0)
    total = kept + swapped(sent, "col", 0)
    distance = 1
    while 1 << distance < count:
        total = total + swapped(total, "col", distance)
        distance += 1
    return total, swapped(total, "col", 0), which


def shards(front, child_tiles, child_rows, child_cols, shift, pivot_tiles):
    local_block = front[0]
    rows_dev, cols_dev = local_block.shape
    row_start = lax.axis_index("row") * rows_dev
    col_start = lax.axis_index("col") * cols_dev
    row_local = child_rows[0] - row_start
    col_local = child_cols[0] - col_start
    count = PANELS * PB // TB
    tiles = pivot_tiles[0][:count]
    pivot_index = (tiles[:, None] * TB + jnp.arange(TB, dtype=jnp.int32)[None, :]).reshape(-1)
    shift_pivots = shift[0][pivot_index][None]

    def placed(start, length):
        local = tiles - start // TB
        inside = (local >= 0) & (local < length // TB)
        return jnp.clip(local, 0, length // TB - 1), inside.astype(jnp.int32)

    def kept(start, length):
        own = (start + jnp.arange(length, dtype=jnp.int32)) // TB
        hit = own[:, None] == tiles[None, :]
        first = ~jnp.any(hit[:, : PB // TB], axis=1)
        return jnp.stack([first, ~jnp.any(hit, axis=1)]).astype(F32)

    keep_row = kept(row_start, rows_dev).T
    keep_col = kept(col_start, cols_dev)
    row_place, row_inside = placed(row_start, rows_dev)
    col_place, col_inside = placed(col_start, cols_dev)

    arrived = [swapped(child_tiles[0, b], "leaf", b) for b in range(2)]
    wide = [widen(arrived[b], col_local[b], cols_dev) for b in range(2)]
    matrix = assemble(local_block, wide, row_local)

    rowpart = strip(matrix, row_place, row_inside, True, "rowstrip")
    corner = strip(rowpart, col_place, col_inside, False, "corner")
    diag = lax.psum(corner, ("row", "col"))
    colpart = strip(matrix, col_place, col_inside, False, "colstrip")
    near, far, which = summed_halves(colpart)
    panel_rows = lax.psum(rowpart, "row")
    inv0, inv1 = invert(diag, shift_pivots)
    factored = eliminate(
        near, far, which[None].astype(jnp.int32), matrix, panel_rows, diag, inv0, inv1,
        keep_row, keep_col,
    )
    return factored[None]


def solution(mesh):
    in_specs = (
        P("leaf", "row", "col"),
        P("leaf", None, "row", "col"),
        P("leaf", None, "row"),
        P("leaf", None, "col"),
        P("leaf", None),
        P("leaf", None),
    )
    out_specs = P("leaf", "row", "col")
    return jax.shard_map(shards, mesh=mesh, in_specs=in_specs, out_specs=out_specs, check_vma=False)
```

time: 1080 us -> 445 us (0.41)
  local copies, waits for them, and re-layouts: 354 us -> 24 us
  other arithmetic: 311 us -> 15.9 us
  Pallas kernels: 0 us -> 116 us
  matrix products: 81.1 us -> 0 us
  waiting for transfers between devices: 299 us -> 263 us
    another operation x34 -> x0, other arithmetic: 238 us -> none  [the longest x30 159 us: invert_block(): factor = jnp.linalg.cholesky(gram)]
    gather x14 -> x1, local copies, waits for them, and re-layouts: 230 us -> 6.15 us  [shards(): shift_pivots = shift[0][pivot_index][None]]
    psum x4 -> x2, waiting for transfers between devices: 223 us -> 59.3 us  [the longest x1 59.3 us: shards(): panel_rows = lax.psum(rowpart, 'row')]
    ppermute x2 -> x5, waiting for transfers between devices: 75.7 us -> 204 us  [swapped(): return lax.ppermute(block, axis, route)]
    pallas_call x0 -> x8, Pallas kernels: none -> 116 us  [the longest x1 34.3 us: eliminate(): pl.pallas_call(functools.partial(eliminate_kernel, blocks), grid_spec=plt...]
    dot_general x4 -> x0, matrix products: 57.9 us -> none  [the longest x2 51.8 us: shards(): jnp.dot(multipliers, panel_rows, preferred_element_type=jnp.float32)]
    select_n x3 -> x0, local copies, waits for them, and re-layouts: 54.4 us -> none  [the longest x2 33.4 us: spread(): picked = jnp.take(arrived, jnp.maximum(row_slots, 0), axis=0)]
    select_n x14 -> x3, other arithmetic: 36.7 us -> 0.04 us  [the longest x2 0.03 us: kept(): own = (start + jnp.arange(length, dtype=jnp.int32)) // TB]
  transfers between devices with their start and end apart: 6 -> 7, of which waited for: 5 -> 4; matrix products, arithmetic and copies ran while one was open for 21% -> 3% of each run, Pallas kernels for 0% -> 8%
where the time goes in v1:
time: 445 us; the launch traced here: 443 us
  waiting for transfers between devices  263 us (59%)
  Pallas kernels  116 us (26%)
  local copies, waits for them, and re-layouts  24 us (5%)
  other arithmetic  15.9 us (4%)
  between operations  13.6 us (3%)
  starting transfers between devices  10.9 us (2%)
    ppermute x5, waiting for transfers between devices, swapped(): return lax.ppermute(block, axis, route)  204 us
    psum x1, waiting for transfers between devices, shards(): panel_rows = lax.psum(rowpart, 'row')  59.3 us
    pallas_call x1, Pallas kernels, eliminate(): pl.pallas_call(functools.partial(eliminate_kernel, blocks), grid_spec=plt...  34.3 us
    pallas_call x1, Pallas kernels, assemble(): pl.pallas_call(functools.partial(assemble_kernel, high), grid=(rows // hi...  31.4 us
    pallas_call x1, Pallas kernels, invert(): pl.pallas_call(invert_kernel, out_shape=[jax.ShapeDtypeStruct((PB, PB), B...  21 us
    pallas_call x2, Pallas kernels, widen(): pl.pallas_call(functools.partial(widen_kernel, width), grid=(cols_dev //...  14.7 us
    pallas_call x3, Pallas kernels, strip(): pl.pallas_call(strip_kernel, grid_spec=pltpu.PrefetchScalarGridSpec(num_s...  14.4 us
    ppermute x5, starting transfers between devices, swapped(): return lax.ppermute(block, axis, route)  10.7 us
  transfers between devices with their start and end apart: 7, of which 4 were waited for; matrix products, arithmetic and copies ran while one was open for 3% of the time, Pallas kernels for 8%

profile of v1, /device:TPU:0, one launch (start us, length us, event | category | flops | bytes accessed | tf_op | source)
XLA Modules:
  0.0 443.4 jit_solution(9851699871202774543)
XLA Ops:
  6.5 0.0 copy-start
  6.5 0.0 copy-start.6
  6.5 0.0 copy-start.8
  6.5 0.0 copy-start.7
  6.5 0.0 all-reduce.5.cloned.1.call-start
  6.6 4.9 %slice_bitcast_fusion = (bf16[768,1536]{1,0:T(8,128)(2,1)}, bf16[768,1536]{1,0:T(8,128)(2,1)}) fusion(bf16[1,2,768,1536]{3,2,1,0:T(8,128)(2,1)} %param.7), kind=kLoop, calls=%fused_computation.2 | loop fusion | bytes 9437184 | tf_op jit(solution)/shard_map/squeeze | solution.py:330
  11.5 4.0 collective-permute-start.1
  15.5 1.6 collective-permute-start
  17.1 0.0 copy-done.6
  17.1 0.0 copy-done.8
  17.2 0.0 copy-done.7
  17.2 100.5 %collective-permute-done.1.tile_ref = bf16[768,1536]{1,0:T(8,128)(2,1)} collective-permute-done((bf16[768,1536]{1,0:T(8,128)(2,1)}, bf16[768,1536]{1,0:T(8,128)(2,1)}, u32[]{:S(2)}, u32[]{:S(2)}) %collective-permute-start.1) | collective-permute-done | bytes 2359328 | tf_op jit(solution)/shard_map/ppermute | solution.py:33
  117.7 0.3 broadcast_in_dim.34.cols_ref
  118.0 8.2 %widen.3.wide1_ref = bf16[768,2048]{1,0:T(8,128)(2,1)} custom-call(s32[1536,128]{1,0:T(8,128)S(1)} %broadcast_in_dim.34.cols_ref, bf16[768,1536]{1,0:T(8,128)(2,1)} %collective-permute-done.1.tile_ref), custom_call_target="tpu_custom_call" | custom-call | flops 4831838208 | bytes 8388608 | tf_op jit(solution)/shard_map/widen/pallas_call | solution.py:48
  126.2 0.0 collective-permute-done.tile_ref
  126.2 0.3 broadcast_in_dim.32.cols_ref
  126.5 6.5 %widen.2.wide0_ref = bf16[768,2048]{1,0:T(8,128)(2,1)} custom-call(s32[1536,128]{1,0:T(8,128)S(1)} %broadcast_in_dim.32.cols_ref, bf16[768,1536]{1,0:T(8,128)(2,1)S(1)} %collective-permute-done.tile_ref), custom_call_target="tpu_custom_call" | custom-call | flops 4831838208 | bytes 8388608 | tf_op jit(solution)/shard_map/widen/pallas_call | solution.py:48
  133.0 0.0 copy-start.5
  133.0 1.9 copy-done.5
  134.9 31.4 %assemble.1.in_ref.front_ref = bf16[4096,2048]{1,0:T(8,128)(2,1)} custom-call(s32[1,768]{1,0:T(1,128)S(1)} %get-tuple-element.18.row0_ref, s32[1,768]{1,0:T(1,128)S(1)} %get-tuple-element.17.row1_ref, bf16[768,2048]{1,0:T(8,128)(2,1)S(1)} %copy-done.5, bf16[768,2048]{1,0:T(8,128)(2,1)} %widen.3.wide1_ref, bf16[4096,2048]{1,0:T(8,128)(2,1)} %bitcast.33), custom_call_target="tpu_custom_call" | custom-call | flops 25769803776 | bytes 33554432 | tf_op jit(solution)/shard_map/assemble/pallas_call | solution.py:86
  166.3 6.5 %colstrip.1 = bf16[4096,1024]{1,0:T(8,128)(2,1)} custom-call(s32[8]{0:T(128)S(1)} %get-tuple-element.20.place_ref, s32[8]{0:T(128)S(1)} %get-tuple-element.23.inside_ref, bf16[4096,2048]{1,0:T(8,128)(2,1)} %assemble.1.in_ref.front_ref), custom_call_target="tpu_custom_call" | custom-call | bytes 16777216 | tf_op jit(solution)/shard_map/colstrip/pallas_call | solution.py:123
  172.8 4.6 %constant_dynamic-slice_fusion = bf16[2048,1024]{1,0:T(8,128)(2,1)} fusion(bf16[4096,1024]{1,0:T(8,128)(2,1)} %colstrip.1, s32[]{:T(128)S(6)} %select_n.44), kind=kLoop, calls=%fused_computation.40 | loop fusion | bytes 8388612 | tf_op jit(solution)/shard_map/dynamic_slice | solution.py:293
  177.4 0.3 collective-permute-start.2
  177.7 7.2 %collective-permute-done.2 = bf16[2048,1024]{1,0:T(8,128)(2,1)} collective-permute-done((bf16[2048,1024]{1,0:T(8,128)(2,1)}, bf16[2048,1024]{1,0:T(8,128)(2,1)}, u32[]{:S(2)}, u32[]{:S(2)}) %collective-permute-start.2) | collective-permute-done | bytes 4194336 | tf_op jit(solution)/shard_map/ppermute | solution.py:33
  184.9 7.5 %dynamic-slice_add_fusion = bf16[2048,1024]{1,0:T(8,128)(2,1)} fusion(bf16[2048,1024]{1,0:T(8,128)(2,1)} %collective-permute-done.2, bf16[4096,1024]{1,0:T(8,128)(2,1)} %colstrip.1, s32[]{:T(128)S(6)} %select_n.43), kind=kLoop, calls=%fused_computation.1 | loop fusion | flops 8388608 | bytes 12582916 | tf_op jit(solution)/shard_map/add | solution.py:294
  192.5 4.8 %collective-permute-start.3 = (bf16[2048,1024]{1,0:T(8,128)(2,1)}, bf16[2048,1024]{1,0:T(8,128)(2,1)}, u32[]{:S(2)}, u32[]{:S(2)}) collective-permute-start(bf16[2048,1024]{1,0:T(8,128)(2,1)} %dynamic-slice_add_fusion), channel_id=1, source_target_pairs={{0,2},{2,0},{1,3},{3,1},{4,6},{6,4},{5,7},{7,5},{8,10},{10,8},{9,1... | collective-permute-start | bytes 12582920 | tf_op jit(solution)/shard_map/ppermute | solution.py:33
  197.3 0.1 broadcast_compare_fusion
  197.4 0.1 slice_reduce_fusion
  197.6 3.1 rowstrip.1.in_ref
  200.8 0.0 copy-start.2
  200.8 2.0 copy-done.2
  202.8 4.7 %corner.1 = bf16[1024,1024]{1,0:T(8,128)(2,1)} custom-call(s32[8]{0:T(128)S(1)} %get-tuple-element.20.place_ref, s32[8]{0:T(128)S(1)} %get-tuple-element.23.inside_ref, bf16[1024,2048]{1,0:T(8,128)(2,1)} %copy-done.2), custom_call_target="tpu_custom_call" | custom-call | bytes 4194304 | tf_op jit(solution)/shard_map/corner/pallas_call | solution.py:123
  207.5 0.0 all-reduce.5.cloned.1.call-update
  207.5 0.2 all-reduce.3.cloned.1.call-start
  207.7 0.1 broadcast_compare_fusion.1
  207.9 0.6 copy.10
  208.6 0.1 iota_add_fusion.2
  208.7 0.0 copy-done
  208.7 6.2 %gather_fusion = f32[1024]{0:T(1024)S(1)} fusion(f32[8192]{0:T(1024)S(1)} %bitcast.28, s32[1024]{0:T(1024)S(1)} %broadcast_clamp_fusion), kind=kCustom, calls=%fused_computation | custom fusion | bytes 12288 | tf_op jit(solution)/shard_map/gather | solution.py:312
  214.9 0.0 all-reduce.3.cloned.1.call-update
  214.9 96.0 %collective-permute-done.3 = bf16[2048,1024]{1,0:T(8,128)(2,1)} collective-permute-done((bf16[2048,1024]{1,0:T(8,128)(2,1)}, bf16[2048,1024]{1,0:T(8,128)(2,1)}, u32[]{:S(2)}, u32[]{:S(2)}) %collective-permute-start.3) | collective-permute-done | bytes 4194336 | tf_op jit(solution)/shard_map/ppermute | solution.py:33
  310.9 7.8 %add.88.near_ref = bf16[2048,1024]{1,0:T(8,128)(2,1)} add(bf16[2048,1024]{1,0:T(8,128)(2,1)} %dynamic-slice_add_fusion, bf16[2048,1024]{1,0:T(8,128)(2,1)} %collective-permute-done.3) | non-fusion elementwise | flops 2097152 | bytes 12582912 | tf_op jit(solution)/shard_map/add | solution.py:297
  318.7 0.0 collective-permute-start.4
  318.7 0.0 all-reduce.5.cloned.1.call-done.diag_ref
  318.7 0.0 copy-start.3
  318.7 1.6 copy-done.3
  320.3 21.0 %invert.1 = (bf16[512,512]{1,0:T(8,128)(2,1)S(1)}, bf16[512,512]{1,0:T(8,128)(2,1)S(1)}) custom-call(bf16[1024,1024]{1,0:T(8,128)(2,1)S(1)} %copy-done.3, f32[1,1024]{1,0:T(1,128)S(1)} %bitcast.30), custom_call_target="tpu_custom_call" | custom-call | flops 64424509440 | bytes 4194304 | tf_op jit(solution)/shard_map/invert/pallas_call | solution.py:198
  341.3 59.3 %all-reduce.3.cloned.1.call-done.rows_ref = bf16[1024,2048]{1,0:T(8,128)(2,1)} async-done(((bf16[1024,2048]{1,0:T(8,128)(2,1)}), bf16[1024,2048]{1,0:T(8,128)(2,1)}) %all-reduce.3.cloned.1.call-update) | async-done | bytes 4194320 | tf_op jit(solution)/shard_map/psum | solution.py:339
  400.7 0.0 collective-permute-done.4.far_ref
  400.7 0.0 copy-start.4
  400.7 1.6 copy-done.4
  402.3 0.0 copy-start.1
  402.3 34.3 %eliminate.1 = bf16[4096,2048]{1,0:T(8,128)(2,1)} custom-call(s32[1]{0:T(128)} %bitcast.half_ref, bf16[2048,1024]{1,0:T(8,128)(2,1)} %add.88.near_ref, bf16[2048,1024]{1,0:T(8,128)(2,1)} %collective-permute-done.4.far_ref, bf16[4096,2048]{1,0:T(8,128)(2,1)} %assemble.1.in_ref.front_ref, bf16[1024,2048]{1,0:T(8,128)(2,1)} %all-reduce.3.cloned.1.call-done.rows_ref, ...), custom_call_target="tpu_custom_call" | custom-call | flops 17179869184 | bytes 50331648 | tf_op jit(solution)/shard_map/eliminate/pallas_call | solution.py:260
  436.6 0.0 copy-done.1
  (22 shorter events, 0.3 us)
Async XLA Ops:
  6.5 202.1 %copy-start = (f32[1,8192]{1,0:T(1,128)S(1)}, f32[1,8192]{1,0:T(1,128)}, u32[]{:S(2)}) copy-start(f32[1,8192]{1,0:T(1,128)} %param.10) | copy-start | bytes 98308
  6.5 10.5 %copy-start.6 = (s32[1,2,1536]{2,1,0:T(2,128)S(1)}, s32[1,2,1536]{2,1,0:T(2,128)}, u32[]{:S(2)}) copy-start(s32[1,2,1536]{2,1,0:T(2,128)} %param.9) | copy-start | bytes 36868
  6.5 10.6 %copy-start.8 = (s32[1,64]{1,0:T(1,128)S(1)}, s32[1,64]{1,0:T(1,128)}, u32[]{:S(2)}) copy-start(s32[1,64]{1,0:T(1,128)} %param.11) | copy-start | bytes 772
  6.5 10.6 %copy-start.7 = (s32[1,2,768]{2,1,0:T(2,128)S(1)}, s32[1,2,768]{2,1,0:T(2,128)}, u32[]{:S(2)}) copy-start(s32[1,2,768]{2,1,0:T(2,128)} %param.8) | copy-start | bytes 18436
  6.5 312.1 %all-reduce.5.cloned.1.call-start = ((), (), s32[]{:S(2)}) async-start(), calls=%async_computation.1 | async-start | bytes 4194304 | tf_op jit(solution)/shard_map/psum | solution.py:336
  11.5 106.3 %collective-permute-start.1 = (bf16[768,1536]{1,0:T(8,128)(2,1)}, bf16[768,1536]{1,0:T(8,128)(2,1)}, u32[]{:S(2)}, u32[]{:S(2)}) collective-permute-start(bf16[768,1536]{1,0:T(8,128)(2,1)} %get-tuple-element.11), channel_id=1, source_target_pairs={{0,16},{16,0},{8,24},{24,8},{1,17},{17,1},{9,25},{25,9},{2,18},{18... | collective-permute-start | bytes 7077896 | tf_op jit(solution)/shard_map/ppermute | solution.py:33
  15.5 110.7 %collective-permute-start = (bf16[768,1536]{1,0:T(8,128)(2,1)}, bf16[768,1536]{1,0:T(8,128)(2,1)S(1)}, u32[]{:S(2)}, u32[]{:S(2)}) collective-permute-start(bf16[768,1536]{1,0:T(8,128)(2,1)} %get-tuple-element.12), channel_id=1, source_target_pairs={{0,8},{8,0},{16,24},{24,16},{1,9},{9,1},{17,25},{25,17},{2,10},{10... | collective-permute-start | bytes 7077896 | tf_op jit(solution)/shard_map/ppermute | solution.py:33
  133.0 1.9 copy-start.5
  177.4 7.5 %collective-permute-start.2 = (bf16[2048,1024]{1,0:T(8,128)(2,1)}, bf16[2048,1024]{1,0:T(8,128)(2,1)}, u32[]{:S(2)}, u32[]{:S(2)}) collective-permute-start(bf16[2048,1024]{1,0:T(8,128)(2,1)} %constant_dynamic-slice_fusion), channel_id=1, source_target_pairs={{0,1},{1,0},{2,3},{3,2},{4,5},{5,4},{6,7},{7,6},{8,9},{9,8},{10,11... | collective-permute-start | bytes 12582920 | tf_op jit(solution)/shard_map/ppermute | solution.py:33
  192.5 118.4 %collective-permute-start.3 = (bf16[2048,1024]{1,0:T(8,128)(2,1)}, bf16[2048,1024]{1,0:T(8,128)(2,1)}, u32[]{:S(2)}, u32[]{:S(2)}) collective-permute-start(bf16[2048,1024]{1,0:T(8,128)(2,1)} %dynamic-slice_add_fusion), channel_id=1, source_target_pairs={{0,2},{2,0},{1,3},{3,1},{4,6},{6,4},{5,7},{7,5},{8,10},{10,8},{9,1... | collective-permute-start | bytes 12582920 | tf_op jit(solution)/shard_map/ppermute | solution.py:33
  200.8 2.0 copy-start.2
  207.5 193.2 %all-reduce.3.cloned.1.call-start = ((), (), s32[]{:S(2)}) async-start(), calls=%async_computation | async-start | bytes 8388608 | tf_op jit(solution)/shard_map/psum | solution.py:339
  318.7 82.0 %collective-permute-start.4 = (bf16[2048,1024]{1,0:T(8,128)(2,1)}, bf16[2048,1024]{1,0:T(8,128)(2,1)}, u32[]{:S(2)}, u32[]{:S(2)}) collective-permute-start(bf16[2048,1024]{1,0:T(8,128)(2,1)} %add.88.near_ref), channel_id=1, source_target_pairs={{0,1},{1,0},{2,3},{3,2},{4,5},{5,4},{6,7},{7,6},{8,9},{9,8},{10,11... | collective-permute-start | bytes 12582920 | tf_op jit(solution)/shard_map/ppermute | solution.py:33
  318.7 1.6 copy-start.3
  400.7 1.6 copy-start.4
  402.3 34.3 %copy-start.1 = (f32[1,8192]{1,0:T(1,128)S(1)}, f32[1,8192]{1,0:T(1,128)}, u32[]{:S(2)}) copy-start(f32[1,8192]{1,0:T(1,128)} %param.10) | copy-start | bytes 98308
Sparse Core Ops, SparseCore 0:
  207.6 82.6 all-reduce.4
  292.7 107.9 all-reduce.2

commit v2 on v1

--- a/solution.py
+++ b/solution.py
@@ -33,7 +33,7 @@
     return lax.ppermute(block, axis, route)
 
 
-def widen_kernel(width, cols_ref, tile_ref, out_ref):
+def widen_kernel(width, cols_ref, tile_ref, ready_ref, out_ref):
     base = pl.program_id(0) * width
     lane = lax.broadcasted_iota(jnp.int32, cols_ref.shape, 1)
     delta = cols_ref[...] - base
@@ -41,7 +41,7 @@
     out_ref[...] = mm(tile_ref[...], jnp.concatenate(picks, axis=1)).astype(BF16)
 
 
-def widen(tile, col_local, cols_dev):
+def widen(tile, col_local, cols_dev, ready):
     height, entries = tile.shape
     width = min(512, cols_dev)
     spread_cols = jnp.broadcast_to(col_local[:, None], (entries, TB))
@@ -51,6 +51,7 @@
         in_specs=[
             pl.BlockSpec((entries, TB), lambda j: (0, 0)),
             pl.BlockSpec((height, entries), lambda j: (0, 0)),
+            pl.BlockSpec(memory_space=pl.ANY),
         ],
         out_specs=pl.BlockSpec((height, width), lambda j: (0, j)),
         out_shape=jax.ShapeDtypeStruct((height, cols_dev), BF16),
@@ -59,7 +60,7 @@
             flops=2 * height * entries * cols_dev, bytes_accessed=8 << 20, transcendentals=0
         ),
         name="widen",
-    )(spread_cols, tile)
+    )(spread_cols, tile, ready)
 
 
 def assemble_kernel(high, row0_ref, row1_ref, wide0_ref, wide1_ref, front_ref, out_ref):
@@ -76,7 +77,7 @@
         out_ref[:, part] = (front_ref[:, part].astype(F32) + landed).astype(BF16)
 
 
-def assemble(front, wide, row_local):
+def assemble(front, wide, row_local, name):
     rows, cols = front.shape
     entries = wide[0].shape[0]
     high = min(512, rows)
@@ -93,11 +94,11 @@
         cost_estimate=pl.CostEstimate(
             flops=4 * rows * entries * cols, bytes_accessed=4 * rows * cols, transcendentals=0
         ),
-        name="assemble",
+        name=name,
     )(row_local[0][None], row_local[1][None], wide[0], wide[1], front)
 
 
-def strip_kernel(place_ref, inside_ref, in_ref, out_ref):
+def strip_kernel(place_ref, inside_ref, half_ref, in_ref, out_ref):
     held = inside_ref[pl.program_id(0)] > 0
 
     @pl.when(held)
@@ -109,21 +110,25 @@
         out_ref[...] = jnp.zeros_like(out_ref)
 
 
-def strip(matrix, place, inside, by_rows, name):
+def strip(matrix, place, inside, by_rows, name, half=None):
     rows, cols = matrix.shape
+    if half is None:
+        half = jnp.int32(0)
+    else:
+        rows = rows // 2
     count = place.shape[0]
     if by_rows:
-        spec = pl.BlockSpec((TB, cols), lambda q, place, inside: (place[q], 0))
-        out = pl.BlockSpec((TB, cols), lambda q, place, inside: (q, 0))
+        spec = pl.BlockSpec((TB, cols), lambda q, place, inside, half: (place[q], 0))
+        out = pl.BlockSpec((TB, cols), lambda q, place, inside, half: (q, 0))
         shape = (count * TB, cols)
     else:
-        spec = pl.BlockSpec((rows, TB), lambda q, place, inside: (0, place[q]))
-        out = pl.BlockSpec((rows, TB), lambda q, place, inside: (0, q))
+        spec = pl.BlockSpec((rows, TB), lambda q, place, inside, half: (half[0], place[q]))
+        out = pl.BlockSpec((rows, TB), lambda q, place, inside, half: (0, q))
         shape = (rows, count * TB)
     return pl.pallas_call(
         strip_kernel,
         grid_spec=pltpu.PrefetchScalarGridSpec(
-            num_scalar_prefetch=2, grid=(count,), in_specs=[spec], out_specs=out
+            num_scalar_prefetch=3, grid=(count,), in_specs=[spec], out_specs=out
         ),
         out_shape=jax.ShapeDtypeStruct(shape, BF16),
         compiler_params=params("arbitrary"),
@@ -131,7 +136,7 @@
             flops=0, bytes_accessed=4 * shape[0] * shape[1], transcendentals=0
         ),
         name=name,
-    )(place, inside, matrix)
+    )(place, inside, half[None].astype(jnp.int32), matrix)
 
 
 def newton_inverse(block, shift_row, x_ref):
@@ -186,7 +191,7 @@
     return x_ref[...].astype(BF16)
 
 
-def invert_kernel(diag_ref, shift_ref, inv0_ref, inv1_ref, x_ref):
+def invert_kernel(diag_ref, shift_ref, ready_ref, inv0_ref, inv1_ref, x_ref):
     inv0 = newton_inverse(diag_ref[:PB, :PB], shift_ref[:, :PB], x_ref)
     inv0_ref[...] = inv0
     below = mm(diag_ref[PB:, :PB], inv0).astype(BF16)
@@ -194,109 +199,130 @@
     inv1_ref[...] = newton_inverse(second.astype(BF16), shift_ref[:, PB:], x_ref)
 
 
-def invert(diag, shift_row):
+def invert(diag, shift_row, ready):
     return pl.pallas_call(
         invert_kernel,
+        in_specs=[
+            pl.BlockSpec(memory_space=pltpu.VMEM),
+            pl.BlockSpec(memory_space=pltpu.VMEM),
+            pl.BlockSpec(memory_space=pl.ANY),
+        ],
         out_shape=[jax.ShapeDtypeStruct((PB, PB), BF16)] * 2,
         scratch_shapes=[pltpu.VMEM((PB, PB), F32)],
         compiler_params=params(),
         cost_estimate=pl.CostEstimate(flops=60 << 30, bytes_accessed=4 << 20, transcendentals=0),
         name="invert",
-    )(diag, shift_row)
+    )(diag, shift_row, ready)
+
+
+def factors_kernel(strip_ref, diag_ref, inv0_ref, inv1_ref, keep_row_ref, out_ref):
+    first = mm(strip_ref[:, :PB], inv0_ref[...]).astype(BF16)
+    lowered = strip_ref[:, PB:].astype(F32) - mm(first, diag_ref[:PB, PB:])
+    second = mm(lowered.astype(BF16), inv1_ref[...]).astype(BF16)
+    out_ref[:, :PB] = (first.astype(F32) * keep_row_ref[:, 0:1]).astype(BF16)
+    out_ref[:, PB:] = (second.astype(F32) * keep_row_ref[:, 1:2]).astype(BF16)
+
+
+def factors(columns, diag, inv0, inv1, keep_row):
+    rows, depth = columns.shape
+    high = min(512, rows)
+    fixed = lambda shape: pl.BlockSpec(shape, lambda i: (0, 0))
+    block = pl.BlockSpec((high, depth), lambda i: (i, 0))
+    return pl.pallas_call(
+        factors_kernel,
+        grid=(rows // high,),
+        in_specs=[
+            block,
+            fixed((depth, depth)),
+            fixed((PB, PB)),
+            fixed((PB, PB)),
+            pl.BlockSpec((high, 2), lambda i: (i, 0)),
+        ],
+        out_specs=block,
+        out_shape=jax.ShapeDtypeStruct((rows, depth), BF16),
+        compiler_params=params("arbitrary"),
+        cost_estimate=pl.CostEstimate(
+            flops=6 * rows * PB * PB, bytes_accessed=4 * rows * depth, transcendentals=0
+        ),
+        name="factors",
+    )(columns, diag, inv0, inv1, keep_row)
 
 
 def eliminate_kernel(
-    blocks, half_ref, near_ref, far_ref, front_ref, rows_ref, diag_ref, inv0_ref, inv1_ref,
-    keep_row_ref, keep_col_ref, out_ref, right, left,
+    left_ref, front_ref, rows_ref, more_ref, diag_ref, inv0_ref, keep_col_ref, out_ref, right
 ):
-    i = pl.program_id(0)
-    inv0 = inv0_ref[...]
     cols = out_ref.shape[1]
     step = min(512, cols)
 
-    @pl.when(i == 0)
+    @pl.when(pl.program_id(0) == 0)
     def _():
-        below = mm(diag_ref[PB:, :PB], inv0).astype(BF16)
+        below = mm(diag_ref[PB:, :PB], inv0_ref[...]).astype(BF16)
         for start in range(0, cols, step):
             part = slice(start, start + step)
-            first = rows_ref[:PB, part]
-            second = rows_ref[PB:, part].astype(F32) - mm(below, first)
+            first = rows_ref[:PB, part] + more_ref[:PB, part]
+            second = rows_ref[PB:, part].astype(F32) + more_ref[PB:, part].astype(F32)
+            second = second - mm(below, first)
             right[:PB, part] = (first.astype(F32) * keep_col_ref[0:1, part]).astype(BF16)
             right[PB:, part] = (
                 second.astype(BF16).astype(F32) * keep_col_ref[1:2, part]
             ).astype(BF16)
 
-    mine = (i // blocks) == half_ref[0]
-
-    def factors(strip_ref):
-        first = mm(strip_ref[:, :PB], inv0).astype(BF16)
-        lowered = strip_ref[:, PB:].astype(F32) - mm(first, diag_ref[:PB, PB:])
-        second = mm(lowered.astype(BF16), inv1_ref[...]).astype(BF16)
-        left[:, :PB] = (first.astype(F32) * keep_row_ref[:, 0:1]).astype(BF16)
-        left[:, PB:] = (second.astype(F32) * keep_row_ref[:, 1:2]).astype(BF16)
-
-    @pl.when(mine)
-    def _():
-        factors(near_ref)
-
-    @pl.when(jnp.logical_not(mine))
-    def _():
-        factors(far_ref)
-
     for start in range(0, cols, step):
         part = slice(start, start + step)
-        update = mm(left[...], right[:, part])
+        update = mm(left_ref[...], right[:, part])
         out_ref[:, part] = (front_ref[:, part].astype(F32) - update).astype(BF16)
 
 
-def eliminate(near, far, half, matrix, panel_rows, diag, inv0, inv1, keep_row, keep_col):
+def eliminate(left, matrix, own_rows, other_rows, diag, inv0, keep_col):
     rows, cols = matrix.shape
-    depth = near.shape[1]
-    high = min(512, near.shape[0])
-    blocks = near.shape[0] // high
-    fixed = lambda shape: pl.BlockSpec(shape, lambda i, half: (0, 0))
-    strip_spec = pl.BlockSpec((high, depth), lambda i, half: (lax.rem(i, blocks), 0))
-    block = pl.BlockSpec((high, cols), lambda i, half: (i, 0))
-    return pl.pallas_call(
-        functools.partial(eliminate_kernel, blocks),
-        grid_spec=pltpu.PrefetchScalarGridSpec(
-            num_scalar_prefetch=1,
-            grid=(rows // high,),
-            in_specs=[
-                strip_spec,
-                strip_spec,
-                block,
-                fixed((depth, cols)),
-                fixed((depth, depth)),
-                fixed((PB, PB)),
-                fixed((PB, PB)),
-                pl.BlockSpec((high, 2), lambda i, half: (i, 0)),
-                fixed((2, cols)),
-            ],
-            out_specs=block,
-            scratch_shapes=[pltpu.VMEM((depth, cols), BF16), pltpu.VMEM((high, depth), BF16)],
-        ),
+    depth = left.shape[1]
+    high = min(512, rows)
+    fixed = lambda shape: pl.BlockSpec(shape, lambda i: (0, 0))
+    block = pl.BlockSpec((high, cols), lambda i: (i, 0))
+    return pl.pallas_call(
+        eliminate_kernel,
+        grid=(rows // high,),
+        in_specs=[
+            pl.BlockSpec((high, depth), lambda i: (i, 0)),
+            block,
+            fixed((depth, cols)),
+            fixed((depth, cols)),
+            fixed((depth, depth)),
+            fixed((PB, PB)),
+            fixed((2, cols)),
+        ],
+        out_specs=block,
         out_shape=jax.ShapeDtypeStruct((rows, cols), BF16),
+        scratch_shapes=[pltpu.VMEM((depth, cols), BF16)],
         compiler_params=params("arbitrary"),
         cost_estimate=pl.CostEstimate(
             flops=2 * rows * depth * cols, bytes_accessed=6 * rows * cols, transcendentals=0
         ),
         name="eliminate",
-    )(half, near, far, matrix, panel_rows, diag, inv0, inv1, keep_row, keep_col)
-
-
-def summed_halves(part):
+    )(left, matrix, own_rows, other_rows, diag, inv0, keep_col)
+
+
+def summed_halves(kept, sent):
     count = lax.axis_size("col")
-    rows = part.shape[0] // 2
     which = lax.axis_index("col") & 1
-    kept = lax.dynamic_slice_in_dim(part, which * rows, rows, 0)
-    sent = lax.dynamic_slice_in_dim(part, (1 - which) * rows, rows, 0)
     total = kept + swapped(sent, "col", 0)
     distance = 1
     while 1 << distance < count:
         total = total + swapped(total, "col", distance)
         distance += 1
-    return total, swapped(total, "col", 0), which
+    other = swapped(total, "col", 0)
+    return jnp.where(which == 0, total, other), jnp.where(which == 0, other, total), total
+
+
+def summed_rows(part):
+    count = lax.axis_size("row")
+    other = jnp.zeros_like(part)
+    distance = 0
+    while 1 << distance < count:
+        part = part if distance == 0 else part + other
+        other = swapped(part, "row", distance)
+        distance += 1
+    return part, other
 
 
 def shards(front, child_tiles, child_rows, child_cols, shift, pivot_tiles):
@@ -327,21 +353,36 @@
     row_place, row_inside = placed(row_start, rows_dev)
     col_place, col_inside = placed(col_start, cols_dev)
 
+    which = lax.axis_index("col") & 1
+    row_tile = row_local // TB
+    hit = row_tile[:, :, None] == (tiles - row_start // TB)[None, None, :]
+    strip_row = jnp.max(
+        jnp.where(hit, jnp.arange(count, dtype=jnp.int32) * TB + (row_local % TB)[:, :, None], -1), axis=2
+    )
+
     arrived = [swapped(child_tiles[0, b], "leaf", b) for b in range(2)]
-    wide = [widen(arrived[b], col_local[b], cols_dev) for b in range(2)]
-    matrix = assemble(local_block, wide, row_local)
-
-    rowpart = strip(matrix, row_place, row_inside, True, "rowstrip")
+    *halves, front_ready = summed_halves(
+        strip(local_block, col_place, col_inside, False, "colstrip", which),
+        strip(local_block, col_place, col_inside, False, "colsent", 1 - which),
+    )
+    front_columns = jnp.concatenate(halves, axis=0)
+    front_rows = strip(local_block, row_place, row_inside, True, "rowstrip")
+
+    wide = [widen(arrived[b], col_local[b], cols_dev, front_ready) for b in range(2)]
+    rowpart = assemble(front_rows, wide, strip_row, "rowpart")
     corner = strip(rowpart, col_place, col_inside, False, "corner")
     diag = lax.psum(corner, ("row", "col"))
-    colpart = strip(matrix, col_place, col_inside, False, "colstrip")
-    near, far, which = summed_halves(colpart)
-    panel_rows = lax.psum(rowpart, "row")
-    inv0, inv1 = invert(diag, shift_pivots)
-    factored = eliminate(
-        near, far, which[None].astype(jnp.int32), matrix, panel_rows, diag, inv0, inv1,
-        keep_row, keep_col,
+    own_rows, other_rows = summed_rows(rowpart)
+    child_strips = [strip(w, col_place, col_inside, False, "childstrip") for w in wide]
+    *child_columns, _ = summed_halves(
+        jnp.where(which == 0, child_strips[0], child_strips[1]),
+        jnp.where(which == 0, child_strips[1], child_strips[0]),
     )
+    matrix = assemble(local_block, wide, row_local, "assemble")
+    columns = assemble(front_columns, child_columns, row_local, "columns")
+    inv0, inv1 = invert(diag, shift_pivots, columns)
+    left = factors(columns, diag, inv0, inv1, keep_row)
+    factored = eliminate(left, matrix, own_rows, other_rows, diag, inv0, keep_col)
     return factored[None]
 
 

time: 445 us -> 361 us (0.81)
  waiting for transfers between devices: 263 us -> 120 us
  Pallas kernels: 116 us -> 157 us
  other arithmetic: 15.9 us -> 41.4 us
  local copies, waits for them, and re-layouts: 24 us -> 16.6 us
    ppermute x5 -> x9, waiting for transfers between devices: 204 us -> 120 us  [swapped(): return lax.ppermute(block, axis, route)]
    psum x1 -> x0, waiting for transfers between devices: 59.3 us -> none  [shards(): panel_rows = lax.psum(rowpart, 'row')]
    pallas_call x1 -> x3, Pallas kernels: 31.4 us -> 59 us  [assemble(): pl.pallas_call(functools.partial(assemble_kernel, high), grid=(rows // hi...]
    select_n x0 -> x5, other arithmetic: none -> 9.36 us  [the longest x1 5.9 us: summed_halves(): jnp.where(which == 0, total, other)]
    pallas_call x3 -> x6, Pallas kernels: 14.4 us -> 22.6 us  [strip(): pl.pallas_call(strip_kernel, grid_spec=pltpu.PrefetchScalarGridSpec(num_s...]
    concatenate x0 -> x1, other arithmetic: none -> 7.93 us  [shards(): front_columns = jnp.concatenate(halves, axis=0)]
    pallas_call x2 -> x3, Pallas kernels: 55.3 us -> 60.9 us  [the longest x1 27.6 us: eliminate(): pl.pallas_call(eliminate_kernel, grid=(rows // high,), in_specs=[pl.Block...]
    dynamic_slice x1 -> x0, local copies, waits for them, and re-layouts: 4.59 us -> none  [summed_halves(): sent = lax.dynamic_slice_in_dim(part, (1 - which) * rows, rows, 0)]
  transfers between devices with their start and end apart: 7 -> 10, of which waited for: 4 -> 4; matrix products, arithmetic and copies ran while one was open for 3% -> 12% of each run, Pallas kernels for 8% -> 32%
where the time goes in v2:
time: 361 us
  Pallas kernels  157 us (43%)
  waiting for transfers between devices  120 us (33%)
  other arithmetic  41.4 us (11%)
  local copies, waits for them, and re-layouts  16.6 us (5%)
  between operations  13.7 us (4%)
  starting transfers between devices  11 us (3%)
    ppermute x9, waiting for transfers between devices, swapped(): return lax.ppermute(block, axis, route)  120 us
    pallas_call x3, Pallas kernels, assemble(): pl.pallas_call(functools.partial(assemble_kernel, high), grid=(rows // hi...  59 us
    pallas_call x1, Pallas kernels, eliminate(): pl.pallas_call(eliminate_kernel, grid=(rows // high,), in_specs=[pl.Block...  27.6 us
    pallas_call x6, Pallas kernels, strip(): pl.pallas_call(strip_kernel, grid_spec=pltpu.PrefetchScalarGridSpec(num_s...  22.6 us
    pallas_call x1, Pallas kernels, invert(): pl.pallas_call(invert_kernel, in_specs=[pl.BlockSpec(memory_space=pltpu.V...  21.1 us
    pallas_call x2, Pallas kernels, widen(): pl.pallas_call(functools.partial(widen_kernel, width), grid=(cols_dev //...  14.7 us
    pallas_call x1, Pallas kernels, factors(): pl.pallas_call(factors_kernel, grid=(rows // high,), in_specs=[block, fix...  12.3 us
    add x2, other arithmetic, summed_halves(): total = total + swapped(total, 'col', distance)  11.3 us
  transfers between devices with their start and end apart: 10, of which 4 were waited for; matrix products, arithmetic and copies ran while one was open for 12% of the time, Pallas kernels for 32%

profile of v2, /device:TPU:0, one launch (start us, length us, event | category | flops | bytes accessed | tf_op | source)
XLA Modules:
  0.0 360.6 jit_solution(8074637185166426367)
XLA Ops:
  6.5 0.0 copy-start
  6.5 0.0 all-reduce.2.cloned.1.call-start
  6.5 0.7 broadcast_multiply_fusion
  7.2 0.7 and_convert_fusion
  7.9 4.3 %colsent.1 = bf16[2048,1024]{1,0:T(8,128)(2,1)S(1)} custom-call(s32[8]{0:T(128)S(1)} %get-tuple-element.30.place_ref, s32[8]{0:T(128)S(1)} %get-tuple-element.31.inside_ref, s32[1]{0:T(128)} %bitcast.6.half_ref, bf16[4096,2048]{1,0:T(8,128)(2,1)} %bitcast.51), custom_call_target="tpu_custom_call" | custom-call | bytes 8388608 | tf_op jit(solution)/shard_map/colsent/pallas_call | solution.py:128
  12.2 2.1 collective-permute-start.1
  14.3 4.6 %colstrip.1 = bf16[2048,1024]{1,0:T(8,128)(2,1)S(1)} custom-call(s32[8]{0:T(128)S(1)} %get-tuple-element.30.place_ref, s32[8]{0:T(128)S(1)} %get-tuple-element.31.inside_ref, s32[1]{0:T(128)} %bitcast.4.half_ref, bf16[4096,2048]{1,0:T(8,128)(2,1)} %bitcast.52), custom_call_target="tpu_custom_call" | custom-call | bytes 8388608 | tf_op jit(solution)/shard_map/colstrip/pallas_call | solution.py:128
  18.9 2.3 collective-permute-done.1
  21.2 6.3 %add.111 = bf16[2048,1024]{1,0:T(8,128)(2,1)} add(bf16[2048,1024]{1,0:T(8,128)(2,1)S(1)} %colstrip.1, bf16[2048,1024]{1,0:T(8,128)(2,1)} %collective-permute-done.1) | non-fusion elementwise | flops 2097152 | bytes 12582912 | tf_op jit(solution)/shard_map/add | solution.py:308
  27.5 2.8 collective-permute-start.2
  30.3 0.0 slice-done
  30.3 0.0 slice-done.1
  30.3 2.5 slice_bitcast_fusion.1
  32.8 1.6 collective-permute-start
  34.4 1.8 collective-permute-start.3
  36.3 0.0 copy-done.11
  36.3 0.1 broadcast_compare_fusion.1
  36.5 0.1 broadcast_compare_fusion
  36.6 0.1 slice_reduce_fusion
  36.8 84.7 %collective-permute-done.2 = bf16[2048,1024]{1,0:T(8,128)(2,1)} collective-permute-done((bf16[2048,1024]{1,0:T(8,128)(2,1)}, bf16[2048,1024]{1,0:T(8,128)(2,1)}, u32[]{:S(2)}, u32[]{:S(2)}) %collective-permute-start.2) | collective-permute-done | bytes 4194336 | tf_op jit(solution)/shard_map/ppermute | solution.py:33
  121.5 7.6 %add.112.ready_ref = bf16[2048,1024]{1,0:T(8,128)(2,1)} add(bf16[2048,1024]{1,0:T(8,128)(2,1)} %add.111, bf16[2048,1024]{1,0:T(8,128)(2,1)} %collective-permute-done.2) | non-fusion elementwise | flops 2097152 | bytes 12582912 | tf_op jit(solution)/shard_map/add | solution.py:311
  129.1 7.5 %collective-permute-done.tile_ref = bf16[768,1536]{1,0:T(8,128)(2,1)S(1)} collective-permute-done((bf16[768,1536]{1,0:T(8,128)(2,1)}, bf16[768,1536]{1,0:T(8,128)(2,1)S(1)}, u32[]{:S(2)}, u32[]{:S(2)}) %collective-permute-start) | collective-permute-done | bytes 2359328 | tf_op jit(solution)/shard_map/ppermute | solution.py:33
  136.6 0.3 broadcast_in_dim.21.cols_ref
  136.9 6.6 %widen.2.in_ref.wide0_ref = bf16[768,2048]{1,0:T(8,128)(2,1)} custom-call(s32[1536,128]{1,0:T(8,128)S(1)} %broadcast_in_dim.21.cols_ref, bf16[768,1536]{1,0:T(8,128)(2,1)S(1)} %collective-permute-done.tile_ref, bf16[2048,1024]{1,0:T(8,128)(2,1)} %add.112.ready_ref), custom_call_target="tpu_custom_call" | custom-call | flops 4831838208 | bytes 8388608 | tf_op jit(solution)/shard_map/widen/pallas_call | solution.py:48
  143.4 1.9 copy-done.3
  145.3 1.5 childstrip.2
  146.8 0.0 collective-permute-done.3.tile_ref
  146.8 0.3 broadcast_in_dim.46.cols_ref
  147.1 8.2 %widen.3.in_ref.wide1_ref = bf16[768,2048]{1,0:T(8,128)(2,1)} custom-call(s32[1536,128]{1,0:T(8,128)S(1)} %broadcast_in_dim.46.cols_ref, bf16[768,1536]{1,0:T(8,128)(2,1)} %collective-permute-done.3.tile_ref, bf16[2048,1024]{1,0:T(8,128)(2,1)} %add.112.ready_ref), custom_call_target="tpu_custom_call" | custom-call | flops 4831838208 | bytes 8388608 | tf_op jit(solution)/shard_map/widen/pallas_call | solution.py:48
  155.3 1.9 copy-done.6
  157.2 1.5 childstrip.3
  158.7 1.3 broadcast_select_fusion.4
  160.0 0.0 collective-permute-start.4
  160.1 2.0 copy.10
  162.1 0.1 iota_add_fusion.2
  162.2 6.2 %gather_fusion = f32[1024]{0:T(1024)S(1)} fusion(f32[8192]{0:T(1024)S(1)} %bitcast.48, s32[1024]{0:T(1024)S(1)} %broadcast_clamp_fusion), kind=kCustom, calls=%fused_computation | custom fusion | bytes 12288 | tf_op jit(solution)/shard_map/gather | solution.py:338
  168.3 0.0 copy-start.10
  168.3 5.1 %rowstrip.1.front_ref = bf16[1024,2048]{1,0:T(8,128)(2,1)S(1)} custom-call(s32[8]{0:T(128)S(1)} %broadcast_clamp_fusion.1.place_ref, s32[8]{0:T(128)S(1)} %get-tuple-element.11.inside_ref, s32[1]{0:T(128)} %constant.93.clone.1.half_ref, bf16[4096,2048]{1,0:T(8,128)(2,1)} %bitcast.53), custom_call_target="tpu_custom_call" | custom-call | bytes 8388608 | tf_op jit(solution)/shard_map/rowstrip/pallas_call | solution.py:128
  173.6 0.6 collective-permute-start.7
  174.1 0.0 collective-permute-done.4
  174.1 4.6 %select_add_fusion = bf16[768,1024]{1,0:T(8,128)(2,1)} fusion(bf16[768,1024]{1,0:T(8,128)(2,1)} %collective-permute-done.4, bf16[768,1024]{1,0:T(8,128)(2,1)S(1)} %childstrip.2, bf16[768,1024]{1,0:T(8,128)(2,1)S(1)} %childstrip.3, pred[]{:T(512)S(6)} %eq.21), kind=kLoop, calls=%fused_computation.6 | loop fusion | flops 1572864 | bytes 6291457 | tf_op jit(solution)/shard_map/add | solution.py:308
  178.7 0.0 copy-done.2
  178.7 0.6 collective-permute-start.5
  179.3 0.1 select_reduce_fusion
  179.5 10.9 %rowpart.1.in_ref.rows_ref = bf16[1024,2048]{1,0:T(8,128)(2,1)} custom-call(s32[1,768]{1,0:T(1,128)S(1)} %get-tuple-element.26.row0_ref, s32[1,768]{1,0:T(1,128)S(1)} %get-tuple-element.25.row1_ref, bf16[768,2048]{1,0:T(8,128)(2,1)S(1)} %copy-done.4, bf16[768,2048]{1,0:T(8,128)(2,1)} %widen.3.in_ref.wide1_ref, bf16[1024,2048]{1,0:T(8,128)(2,1)} %copy-done.2), custom_call_target="tpu_custom_call" | custom-call | flops 6442450944 | bytes 8388608 | tf_op jit(solution)/shard_map/rowpart/pallas_call | solution.py:87
  190.5 5.6 %corner.1 = bf16[1024,1024]{1,0:T(8,128)(2,1)} custom-call(s32[8]{0:T(128)S(1)} %get-tuple-element.30.place_ref, s32[8]{0:T(128)S(1)} %get-tuple-element.31.inside_ref, s32[1]{0:T(128)} %constant.93.clone.1.half_ref, bf16[1024,2048]{1,0:T(8,128)(2,1)} %rowpart.1.in_ref.rows_ref), custom_call_target="tpu_custom_call" | custom-call | bytes 4194304 | tf_op jit(solution)/shard_map/corner/pallas_call | solution.py:128
  196.1 1.5 collective-permute-start.8
  197.6 0.0 all-reduce.2.cloned.1.call-update
  197.6 25.9 %collective-permute-done.5 = bf16[768,1024]{1,0:T(8,128)(2,1)} collective-permute-done((bf16[768,1024]{1,0:T(8,128)(2,1)}, bf16[768,1024]{1,0:T(8,128)(2,1)}, u32[]{:S(2)}, u32[]{:S(2)}) %collective-permute-start.5) | collective-permute-done | bytes 1572896 | tf_op jit(solution)/shard_map/ppermute | solution.py:33
  223.5 3.7 %add.114 = bf16[768,1024]{1,0:T(8,128)(2,1)} add(bf16[768,1024]{1,0:T(8,128)(2,1)} %select_add_fusion, bf16[768,1024]{1,0:T(8,128)(2,1)} %collective-permute-done.5) | non-fusion elementwise | flops 786432 | bytes 4718592 | tf_op jit(solution)/shard_map/add | solution.py:311
  227.2 0.0 collective-permute-start.6
  227.2 31.3 %assemble.1.front_ref = bf16[4096,2048]{1,0:T(8,128)(2,1)} custom-call(s32[1,768]{1,0:T(1,128)S(1)} %get-tuple-element.28.row0_ref, s32[1,768]{1,0:T(1,128)S(1)} %get-tuple-element.27.row1_ref, bf16[768,2048]{1,0:T(8,128)(2,1)S(1)} %copy-done.5, bf16[768,2048]{1,0:T(8,128)(2,1)} %widen.3.in_ref.wide1_ref, bf16[4096,2048]{1,0:T(8,128)(2,1)} %bitcast.54), custom_call_target="tpu_custom_call" | custom-call | flops 25769803776 | bytes 33554432 | tf_op jit(solution)/shard_map/assemble/pallas_call | solution.py:87
  258.5 0.0 collective-permute-done.7
  258.5 5.9 %broadcast_select_fusion.1 = (bf16[2048,1024]{1,0:T(8,128)(2,1)}, bf16[2048,1024]{1,0:T(8,128)(2,1)}) fusion(bf16[2048,1024]{1,0:T(8,128)(2,1)} %add.112.ready_ref, bf16[2048,1024]{1,0:T(8,128)(2,1)} %collective-permute-done.7, pred[]{:T(512)S(6)} %eq.21), kind=kLoop, calls=%fused_computation.3 | loop fusion | flops 4194304 | bytes 16777216 | tf_op jit(solution)/shard_map/jit(_where)/select_n | solution.py:314
  264.4 7.9 %pad_maximum_fusion.front_ref = bf16[4096,1024]{1,0:T(8,128)(2,1)} fusion(bf16[2048,1024]{1,0:T(8,128)(2,1)} %get-tuple-element.16, bf16[2048,1024]{1,0:T(8,128)(2,1)} %get-tuple-element.15), kind=kLoop, calls=%fused_computation.1 | loop fusion | flops 16777216 | bytes 16777216 | tf_op jit(solution)/shard_map/concatenate | solution.py:368
  272.4 0.0 collective-permute-done.6
  272.4 2.1 broadcast_select_fusion.2
  274.5 16.7 %columns.1.ready_ref.strip_ref = bf16[4096,1024]{1,0:T(8,128)(2,1)} custom-call(s32[1,768]{1,0:T(1,128)S(1)} %get-tuple-element.28.row0_ref, s32[1,768]{1,0:T(1,128)S(1)} %get-tuple-element.27.row1_ref, bf16[768,1024]{1,0:T(8,128)(2,1)S(1)} %get-tuple-element.20.wide0_ref, bf16[768,1024]{1,0:T(8,128)(2,1)S(1)} %get-tuple-element.19.wide1_ref, ...), custom_call_target="tpu_custom_call" | custom-call | flops 12884901888 | bytes 16777216 | tf_op jit(solution)/shard_map/columns/pallas_call | solution.py:87
  291.2 1.6 copy-done.8
  292.8 21.1 %invert.1 = (bf16[512,512]{1,0:T(8,128)(2,1)S(1)}, bf16[512,512]{1,0:T(8,128)(2,1)S(1)}) custom-call(bf16[1024,1024]{1,0:T(8,128)(2,1)S(1)} %copy-done.8, f32[1,1024]{1,0:T(1,128)S(1)} %bitcast.50, bf16[4096,1024]{1,0:T(8,128)(2,1)} %columns.1.ready_ref.strip_ref), custom_call_target="tpu_custom_call" | custom-call | flops 64424509440 | bytes 4194304 | tf_op jit(solution)/shard_map/invert/pallas_call | solution.py:203
  313.9 0.0 copy-done.7
  313.9 12.3 %factors.1.left_ref = bf16[4096,1024]{1,0:T(8,128)(2,1)} custom-call(bf16[4096,1024]{1,0:T(8,128)(2,1)} %columns.1.ready_ref.strip_ref, bf16[1024,1024]{1,0:T(8,128)(2,1)S(1)} %copy-done.8, bf16[512,512]{1,0:T(8,128)(2,1)S(1)} %get-tuple-element.7.inv0_ref, bf16[512,512]{1,0:T(8,128)(2,1)S(1)} %get-tuple-element.8.inv1_ref, f32[4096,2]{1,0:T(8,128)S(1)} %bitcast.49), custom_call_target="tpu_custom_call" | custom-call | flops 6442450944 | bytes 16777216 | tf_op jit(solution)/shard_map/factors/pallas_call | solution.py:231
  326.1 0.0 collective-permute-done.8.more_ref
  326.1 27.6 %eliminate.1 = bf16[4096,2048]{1,0:T(8,128)(2,1)} custom-call(bf16[4096,1024]{1,0:T(8,128)(2,1)} %factors.1.left_ref, bf16[4096,2048]{1,0:T(8,128)(2,1)} %assemble.1.front_ref, bf16[1024,2048]{1,0:T(8,128)(2,1)} %rowpart.1.in_ref.rows_ref, bf16[1024,2048]{1,0:T(8,128)(2,1)} %collective-permute-done.8.more_ref, bf16[1024,1024]{1,0:T(8,128)(2,1)S(1)} %copy-done.8, ...), custom_call_target="tpu_custom_call" | custom-call | flops 17179869184 | bytes 50331648 | tf_op jit(solution)/shard_map/eliminate/pallas_call | solution.py:282
  (44 shorter events, 0.4 us)
Async XLA Ops:
  6.5 155.6 %copy-start = (f32[1,8192]{1,0:T(1,128)S(1)}, f32[1,8192]{1,0:T(1,128)}, u32[]{:S(2)}) copy-start(f32[1,8192]{1,0:T(1,128)} %param.10) | copy-start | bytes 98308
  6.5 284.7 %all-reduce.2.cloned.1.call-start = ((), (), s32[]{:S(2)}) async-start(), calls=%async_computation | async-start | bytes 4194304 | tf_op jit(solution)/shard_map/psum | solution.py:374
  12.2 9.0 %collective-permute-start.1 = (bf16[2048,1024]{1,0:T(8,128)(2,1)S(1)}, bf16[2048,1024]{1,0:T(8,128)(2,1)}, u32[]{:S(2)}, u32[]{:S(2)}) collective-permute-start(bf16[2048,1024]{1,0:T(8,128)(2,1)S(1)} %colsent.1), channel_id=1, source_target_pairs={{0,1},{1,0},{2,3},{3,2},{4,5},{5,4},{6,7},{7,6},{8,9},{9,8},{10,11... | collective-permute-start | bytes 12582920 | tf_op jit(solution)/shard_map/ppermute | solution.py:33
  14.3 16.0 %slice-start = ((s8[4718592]{0:T(1024)(128)(4,1)}), s8[4194304]{0:T(1024)(128)(4,1)S(1)}, s32[]{:S(2)}) async-start(s8[4718592]{0:T(1024)(128)(4,1)} %bitcast.55), calls=%async_computation.1 | async-start | bytes 8388608
  14.3 16.0 %slice-start.1 = ((s8[4718592]{0:T(1024)(128)(4,1)}), s8[524288]{0:T(1024)(128)(4,1)S(1)}, s32[]{:S(2)}) async-start(s8[4718592]{0:T(1024)(128)(4,1)} %bitcast.55), calls=%async_computation.2 | async-start | bytes 1048576
  27.5 8.8 %copy-start.11 = (s32[1,64]{1,0:T(1,128)S(1)}, s32[1,64]{1,0:T(1,128)}, u32[]{:S(2)}) copy-start(s32[1,64]{1,0:T(1,128)} %param.11) | copy-start | bytes 772
  27.5 9.3 %copy-start.9 = (s32[1,2,1536]{2,1,0:T(2,128)S(1)}, s32[1,2,1536]{2,1,0:T(2,128)}, u32[]{:S(2)}) copy-start(s32[1,2,1536]{2,1,0:T(2,128)} %param.9) | copy-start | bytes 36868
  27.5 94.0 %collective-permute-start.2 = (bf16[2048,1024]{1,0:T(8,128)(2,1)}, bf16[2048,1024]{1,0:T(8,128)(2,1)}, u32[]{:S(2)}, u32[]{:S(2)}) collective-permute-start(bf16[2048,1024]{1,0:T(8,128)(2,1)} %add.111), channel_id=1, source_target_pairs={{0,2},{2,0},{1,3},{3,1},{4,6},{6,4},{5,7},{7,5},{8,10},{10,8},{9,1... | collective-permute-start | bytes 12582920 | tf_op jit(solution)/shard_map/ppermute | solution.py:33
  32.8 103.8 %collective-permute-start = (bf16[768,1536]{1,0:T(8,128)(2,1)}, bf16[768,1536]{1,0:T(8,128)(2,1)S(1)}, u32[]{:S(2)}, u32[]{:S(2)}) collective-permute-start(bf16[768,1536]{1,0:T(8,128)(2,1)} %get-tuple-element.17), channel_id=1, source_target_pairs={{0,8},{8,0},{16,24},{24,16},{1,9},{9,1},{17,25},{25,17},{2,10},{10... | collective-permute-start | bytes 7077896 | tf_op jit(solution)/shard_map/ppermute | solution.py:33
  34.4 112.4 %collective-permute-start.3 = (bf16[768,1536]{1,0:T(8,128)(2,1)}, bf16[768,1536]{1,0:T(8,128)(2,1)}, u32[]{:S(2)}, u32[]{:S(2)}) collective-permute-start(bf16[768,1536]{1,0:T(8,128)(2,1)} %get-tuple-element.18), channel_id=1, source_target_pairs={{0,16},{16,0},{8,24},{24,8},{1,17},{17,1},{9,25},{25,9},{2,18},{18... | collective-permute-start | bytes 7077896 | tf_op jit(solution)/shard_map/ppermute | solution.py:33
  143.4 1.9 copy-start.3
  155.3 1.9 copy-start.6
  160.0 14.1 %collective-permute-start.4 = (bf16[768,1024]{1,0:T(8,128)(2,1)}, bf16[768,1024]{1,0:T(8,128)(2,1)}, u32[]{:S(2)}, u32[]{:S(2)}) collective-permute-start(bf16[768,1024]{1,0:T(8,128)(2,1)} %broadcast_select_fusion.4), channel_id=1, source_target_pairs={{0,1},{1,0},{2,3},{3,2},{4,5},{5,4},{6,7},{7,6},{8,9},{9,8},{10,11... | collective-permute-start | bytes 4718600 | tf_op jit(solution)/shard_map/ppermute | solution.py:33
  168.3 5.2 %copy-start.10 = (s32[1,2,768]{2,1,0:T(2,128)S(1)}, s32[1,2,768]{2,1,0:T(2,128)}, u32[]{:S(2)}) copy-start(s32[1,2,768]{2,1,0:T(2,128)} %param.8) | copy-start | bytes 18436
  173.5 5.2 %copy-start.2 = (bf16[1024,2048]{1,0:T(8,128)(2,1)}, bf16[1024,2048]{1,0:T(8,128)(2,1)S(1)}, u32[]{:S(2)}) copy-start(bf16[1024,2048]{1,0:T(8,128)(2,1)S(1)} %rowstrip.1.front_ref) | copy-start | bytes 12582916
  173.6 5.9 %copy-start.4 = (bf16[768,2048]{1,0:T(8,128)(2,1)S(1)}, bf16[768,2048]{1,0:T(8,128)(2,1)}, u32[]{:S(2)}) copy-start(bf16[768,2048]{1,0:T(8,128)(2,1)} %widen.2.in_ref.wide0_ref) | copy-start | bytes 9437188
  173.6 85.0 %collective-permute-start.7 = (bf16[2048,1024]{1,0:T(8,128)(2,1)}, bf16[2048,1024]{1,0:T(8,128)(2,1)}, u32[]{:S(2)}, u32[]{:S(2)}) collective-permute-start(bf16[2048,1024]{1,0:T(8,128)(2,1)} %add.112.ready_ref), channel_id=1, source_target_pairs={{0,1},{1,0},{2,3},{3,2},{4,5},{5,4},{6,7},{7,6},{8,9},{9,8},{10,11... | collective-permute-start | bytes 12582920 | tf_op jit(solution)/shard_map/ppermute | solution.py:33
  178.7 44.8 %collective-permute-start.5 = (bf16[768,1024]{1,0:T(8,128)(2,1)}, bf16[768,1024]{1,0:T(8,128)(2,1)}, u32[]{:S(2)}, u32[]{:S(2)}) collective-permute-start(bf16[768,1024]{1,0:T(8,128)(2,1)} %select_add_fusion), channel_id=1, source_target_pairs={{0,2},{2,0},{1,3},{3,1},{4,6},{6,4},{5,7},{7,5},{8,10},{10,8},{9,1... | collective-permute-start | bytes 4718600 | tf_op jit(solution)/shard_map/ppermute | solution.py:33
  196.1 31.2 %copy-start.5 = (bf16[768,2048]{1,0:T(8,128)(2,1)S(1)}, bf16[768,2048]{1,0:T(8,128)(2,1)}, u32[]{:S(2)}) copy-start(bf16[768,2048]{1,0:T(8,128)(2,1)} %widen.2.in_ref.wide0_ref) | copy-start | bytes 9437188
  196.1 130.1 %collective-permute-start.8 = (bf16[1024,2048]{1,0:T(8,128)(2,1)}, bf16[1024,2048]{1,0:T(8,128)(2,1)}, u32[]{:S(2)}, u32[]{:S(2)}) collective-permute-start(bf16[1024,2048]{1,0:T(8,128)(2,1)} %rowpart.1.in_ref.rows_ref), channel_id=1, source_target_pairs={{0,4},{4,0},{1,5},{5,1},{2,6},{6,2},{3,7},{7,3},{8,12},{12,8},{9,1... | collective-permute-start | bytes 12582920 | tf_op jit(solution)/shard_map/ppermute | solution.py:33
  227.2 45.1 %collective-permute-start.6 = (bf16[768,1024]{1,0:T(8,128)(2,1)}, bf16[768,1024]{1,0:T(8,128)(2,1)}, u32[]{:S(2)}, u32[]{:S(2)}) collective-permute-start(bf16[768,1024]{1,0:T(8,128)(2,1)} %add.114), channel_id=1, source_target_pairs={{0,1},{1,0},{2,3},{3,2},{4,5},{5,4},{6,7},{7,6},{8,9},{9,8},{10,11... | collective-permute-start | bytes 4718600 | tf_op jit(solution)/shard_map/ppermute | solution.py:33
  291.2 1.6 copy-start.8
  292.8 21.1 %copy-start.7 = (f32[2,4096]{0,1:T(8,128)S(1)}, f32[2,4096]{0,1:T(8,128)}, u32[]{:S(2)}) copy-start(f32[2,4096]{0,1:T(8,128)} %copy.10) | copy-start | bytes 98308
  326.1 27.6 %copy-start.1 = (f32[1,8192]{1,0:T(1,128)S(1)}, f32[1,8192]{1,0:T(1,128)}, u32[]{:S(2)}) copy-start(f32[1,8192]{1,0:T(1,128)} %param.10) | copy-start | bytes 98308
Sparse Core Ops, SparseCore 0:
  197.7 78.6 all-reduce.1
